TPU v7x, 128 devices: a whole 4x4x4 slice. The times are simulated.
128 devices in a mesh: replica: 8 (over x, core), shard: 16 (over z, y).
Axes of the slice: x: 4, y: 4, z: 4, core: 2. Of those that a mesh axis runs over, the one named last changes fastest.
Arguments:
- activations: bfloat16 [32768, 4096], P(('replica', 'shard')), may hold values from -6 to 6
- output_grads: bfloat16 [32768, 8192], P('replica', 'shard'), may hold values from -0.099609375 to 0.099609375
- error_buffer: float32 [8, 4096, 8192], P('replica', None, 'shard'), may hold values from -3 to 3
- previous_factor: float32 [8192, 32], P('shard'), may hold values from -0.0625 to 0.0625
Outputs:
- new_errors: float32 [8, 4096, 8192], P('replica', None, 'shard')
- basis: float32 [4096, 32], replicated
- right_factor: float32 [8192, 32], P('shard')
All inputs are finite; a program needn't handle non-finite values.
Results may differ from a plain program's by a relative error of at most 0.0003.
Values may be sent and summed in bfloat16 or wider, within the bound.
No kernel may reach another device: no remote copies, remote signals or barrier semaphores. Data moves between devices by JAX's collectives and lax.ppermute only.
A program may use at most 128 MiB of HBM per device.

v0:
```python
import jax
import jax.numpy as jnp
from jax import lax
from jax.sharding import PartitionSpec as P


def local(activations, output_grads, error_buffer, previous_factor):
    grad = lax.dot_general(
        lax.all_gather(activations, "shard", axis=0, tiled=True),
        output_grads,
        (((0,), (0,)), ((), ())),
        preferred_element_type=jnp.float32,
    )
    matrix = error_buffer[0] + grad
    partial_value = jnp.dot(matrix, previous_factor, precision=lax.Precision.HIGHEST)
    left = lax.psum(partial_value, ("replica", "shard"))
    gram = jnp.dot(left.T, left, precision=lax.Precision.HIGHEST)
    lower_factor = jnp.linalg.cholesky(gram)
    basis = lax.linalg.triangular_solve(
        lower_factor, left, left_side=False, lower=True, transpose_a=True
    )
    right_terms = jnp.dot(matrix.T, basis, precision=lax.Precision.HIGHEST)
    right_factor = lax.psum(right_terms, "replica") / lax.axis_size("replica")
    update = jnp.dot(basis, right_factor.T, precision=lax.Precision.HIGHEST)
    new_errors = (matrix - update)[None]
    return (new_errors, basis, right_factor)


def solution(mesh):
    placed = (
        P(("replica", "shard"), None),
        P("replica", "shard"),
        P("replica", None, "shard"),
        P("shard", None),
    )
    return jax.shard_map(
        local,
        mesh=mesh,
        in_specs=placed,
        out_specs=(P("replica", None, "shard"), P(), P("shard", None)),
        check_vma=False,
    )
```

profile of v0, /device:TPU:1, one launch (start us, length us, event | category | flops | bytes accessed | tf_op | source)
XLA Modules:
  0.0 486.8 jit_solution(16707454828789024545)
XLA Ops:
  7.2 0.0 copy-start
  7.2 0.0 all-gather.2.cloned.1.call-start
  7.2 0.7 all-gather.2.cloned.1.call-update
  7.9 0.0 all-reduce.3.cloned.1.call-start
  8.0 202.6 %all-gather.2.cloned.1.call-done = bf16[4096,4096]{1,0:T(8,128)(2,1)} async-done(((bf16[256,4096]{1,0:T(8,128)(2,1)}), bf16[4096,4096]{1,0:T(8,128)(2,1)}) %all-gather.2.cloned.1.call-update) | async-done | bytes 33554448 | tf_op jit(solution)/shard_map/all_gather | solution.py:9
  210.6 28.0 %bitcast_add_fusion = f32[4096,512]{1,0:T(8,128)} fusion(f32[1,4096,512]{2,1,0:T(8,128)} %param.6, bf16[4096,4096]{1,0:T(8,128)(2,1)} %all-gather.2.cloned.1.call-done, bf16[4096,512]{1,0:T(8,128)(2,1)} %param.5), kind=kOutput, calls=%fused_computation | convolution fusion | flops 17181966336 | bytes 54525952 | tf_op jit(solution)/shard_map/dot_general | solution.py:8
  238.7 10.8 %fusion.4 = f32[4096,32]{0,1:T(8,128)} fusion(f32[4096,512]{1,0:T(8,128)} %bitcast_add_fusion, f32[512,32]{0,1:T(8,128)S(1)} %copy-done), kind=kOutput, calls=%fused_computation.13 | convolution fusion | flops 805306368 | bytes 8978432 | tf_op jit(solution)/shard_map/dot_general | solution.py:15
  249.4 0.0 all-reduce.3.cloned.1.call-update
  249.5 0.2 all-reduce.5.cloned.1.call-start
  249.7 144.8 %all-reduce.3.cloned.1.call-done = f32[4096,32]{0,1:T(8,128)} async-done(((f32[4096,32]{0,1:T(8,128)}), f32[4096,32]{0,1:T(8,128)}) %all-reduce.3.cloned.1.call-update) | async-done | bytes 524304 | tf_op jit(solution)/shard_map/psum | solution.py:16
  394.5 1.8 fusion.5
  396.2 0.1 copy.7
  396.3 2.9 cholesky.16
  399.3 0.6 compare_reduce_fusion
  399.9 0.7 fusion
  400.6 2.4 custom-call.6
  403.0 1.7 fusion.1
  404.7 0.0 copy-start.1
  404.7 8.2 %fusion.6 = f32[512,32]{0,1:T(8,128)} fusion(f32[4096,512]{1,0:T(8,128)} %bitcast_add_fusion, f32[4096,32]{0,1:T(8,128)S(1)} %fusion.1), kind=kOutput, calls=%fused_computation.15 | convolution fusion | flops 805306368 | bytes 8978432 | tf_op jit(solution)/shard_map/dot_general | solution.py:22
  412.9 0.0 all-reduce.5.cloned.1.call-update
  412.9 55.2 %all-reduce.5.cloned.1.call-done = f32[512,32]{0,1:T(8,128)} async-done(((f32[512,32]{0,1:T(8,128)}), f32[512,32]{0,1:T(8,128)}) %all-reduce.5.cloned.1.call-update) | async-done | bytes 65552 | tf_op jit(solution)/shard_map/psum | solution.py:23
  468.1 0.8 broadcast_multiply_fusion
  469.0 11.3 %subtract_bitcast_fusion = f32[1,4096,512]{2,1,0:T(8,128)} fusion(f32[4096,512]{1,0:T(8,128)} %bitcast_add_fusion, f32[4096,32]{0,1:T(8,128)S(1)} %fusion.1, f32[512,32]{0,1:T(8,128)S(1)} %broadcast_multiply_fusion), kind=kOutput, calls=%fused_computation.1 | convolution fusion | flops 807403520 | bytes 17367040 | tf_op jit(solution)/shard_map/dot_general | solution.py:24
  480.2 0.0 copy-done.2
  (5 shorter events, 0.0 us)
Async XLA Ops:
  7.2 231.5 %copy-start = (f32[512,32]{0,1:T(8,128)S(1)}, f32[512,32]{0,1:T(8,128)}, u32[]{:S(2)}) copy-start(f32[512,32]{0,1:T(8,128)} %param.7) | copy-start | bytes 196612
  7.2 203.4 %all-gather.2.cloned.1.call-start = ((), (), s32[]{:S(2)}) async-start(), calls=%async_computation | async-start | bytes 35651584 | tf_op jit(solution)/shard_map/all_gather | solution.py:9
  7.9 386.5 %all-reduce.3.cloned.1.call-start = ((), (), s32[]{:S(2)}) async-start(), calls=%async_computation.1 | async-start | bytes 1048576 | tf_op jit(solution)/shard_map/psum | solution.py:16
  249.5 218.7 %all-reduce.5.cloned.1.call-start = ((), (), s32[]{:S(2)}) async-start(), calls=%async_computation.2 | async-start | bytes 131072 | tf_op jit(solution)/shard_map/psum | solution.py:23
  404.7 75.5 %copy-start.1 = (f32[4096,32]{0,1:T(8,128)}, f32[4096,32]{0,1:T(8,128)S(1)}, u32[]{:S(2)}) copy-start(f32[4096,32]{0,1:T(8,128)S(1)} %fusion.1) | copy-start | bytes 1572868
  469.0 11.3 %copy-start.2 = (f32[512,32]{0,1:T(8,128)}, f32[512,32]{0,1:T(8,128)S(1)}, u32[]{:S(2)}) copy-start(f32[512,32]{0,1:T(8,128)S(1)} %broadcast_multiply_fusion) | copy-start | bytes 196612
Sparse Core Ops, SparseCore 0:
  10.2 200.4 all-gather.1
  249.6 144.8 all-reduce.2
  413.0 55.0 all-reduce.4
where the time goes:
time: 488 us; the launch traced here: 487 us
  waiting for transfers between devices  403 us (83%)
  matrix products  61.7 us (13%)
  between operations  13.8 us (3%)
  other arithmetic  7.53 us (2%)
    all_gather x1, waiting for transfers between devices, local(): lax.all_gather(activations, 'shard', axis=0, tiled=True)  203 us
    psum x1, waiting for transfers between devices, local(): left = lax.psum(partial_value, ('replica', 'shard'))  145 us
    psum x1, waiting for transfers between devices, local(): right_factor = lax.psum(right_terms, 'replica') / lax.axis_size('replica')  55.2 us
    dot_general x1, matrix products, local(): lax.dot_general(lax.all_gather(activations, 'shard', axis=0, tiled=True),...  28 us
    dot_general x1, matrix products, local(): update = jnp.dot(basis, right_factor.T, precision=lax.Precision.HIGHEST)  11.3 us
    dot_general x1, matrix products, local(): jnp.dot(matrix, previous_factor, precision=lax.Precision.HIGHEST)  10.8 us
  transfers between devices with their start and end apart: 3, of which 3 were waited for; matrix products, arithmetic and copies ran while one was open for 0% of the time, Pallas kernels for 0%

commit v1 on v0

v1 whole, which is shorter than its diff:
```python
import jax
import jax.numpy as jnp
from jax import lax
from jax.sharding import PartitionSpec as P

ALL = ("replica", "shard")
NX, NC, NZ, NY = 4, 2, 4, 4
HI = lax.Precision.HIGHEST


def pairs(move):
    out = []
    for x in range(NX):
        for c in range(NC):
            for z in range(NZ):
                for y in range(NY):
                    a, b, d, e = move(x, c, z, y)
                    out.append((((x * NC + c) * NZ + z) * NY + y, ((a * NC + b) * NZ + d) * NY + e))
    return out


def inner(v):
    return v ^ 1


def outer(v):
    return 3 - v


def on_p(f):
    return pairs(lambda x, c, z, y: (x, c, z, f(y)) if c == 0 else (x, c, f(z), y))


def on_q(f):
    return pairs(lambda x, c, z, y: (x, c, f(z), y) if c == 0 else (x, c, z, f(y)))


PIN, POUT, QIN, QOUT = on_p(inner), on_p(outer), on_q(inner), on_q(outer)
XIN = pairs(lambda x, c, z, y: (inner(x), c, z, y))
XOUT = pairs(lambda x, c, z, y: (outer(x), c, z, y))
CORE = pairs(lambda x, c, z, y: (x, 1 - c, z, y))


def send(a, perm):
    return lax.ppermute(a, ALL, perm)


def split3(a):
    hi = lax.reduce_precision(a, 8, 7)
    mid = lax.reduce_precision(a - hi, 8, 7)
    lo = lax.reduce_precision(a - hi - mid, 8, 7)
    return jnp.concatenate([hi, mid, lo], 0).astype(jnp.bfloat16)


def exact_dot(a32, b16, dims):
    r = lax.dot_general(split3(a32), b16, (dims, ((), ())), preferred_element_type=jnp.float32)
    n = a32.shape[0]
    return r[:n] + r[n : 2 * n] + r[2 * n :]


def halve(a, bit, perm):
    mine = jnp.where(bit, a[1], a[0])
    other = jnp.where(bit, a[0], a[1])
    return mine + send(other, perm)


def double(a, bit, perm):
    b = send(a, perm)
    return jnp.where(bit, jnp.stack([b, a]), jnp.stack([a, b]))


def by_code(a):
    return a[jnp.array([0, 1, 3, 2])].reshape((2, 2) + a.shape[1:])


def local(activations, output_grads, error_buffer, previous_factor):
    errors = error_buffer[0]
    rep, sh = lax.axis_index("replica"), lax.axis_index("shard")
    x, core = rep // 2, rep % 2
    z, y = sh // 4, sh % 4
    p = jnp.where(core == 0, y, z)
    q = jnp.where(core == 0, z, y)

    def bits(v):
        return v // 2 == 1, (v == 1) | (v == 2)

    (hp, cp), (hq, cq), (hx, cx) = bits(p), bits(q), bits(x)

    gathered = lax.all_gather(activations, "shard", axis=0, tiled=True)

    factor_t = previous_factor.T
    u = exact_dot(factor_t, output_grads, ((1,), (1,)))
    u = u.reshape(32, 4, 4, 256).transpose(1, 2, 0, 3)
    u = jnp.where(core == 0, u, u.swapaxes(0, 1))
    u = u[jnp.array([0, 1, 3, 2])][:, jnp.array([0, 1, 3, 2])].reshape(2, 2, 2, 2, 32, 256)
    u = halve(u, hq, QOUT)
    u = halve(u.swapaxes(0, 1), hp, POUT)
    u = halve(u, cq, QIN)
    u = halve(u, cp, PIN)

    left = exact_dot(u, activations, ((1,), (0,)))
    left = left + lax.dot_general(factor_t, errors, (((1,), (1,)), ((), ())), precision=HI)
    left = left.reshape(32, 8, 512).swapaxes(0, 1).reshape(2, 2, 2, 32, 512)
    left = halve(left, core == 1, CORE)
    left = halve(left, hx, XOUT)
    left = halve(left, cx, XIN)
    for perm in (PIN, QIN, POUT, QOUT):
        left = left + send(left, perm)
    left = double(left, cx, XIN)
    left = double(left, hx, XOUT)
    left = double(left, core == 1, CORE).reshape(8, 32, 512)
    left = left.swapaxes(0, 1).reshape(32, 4096)

    gram = lax.dot_general(left, left, (((1,), (1,)), ((), ())), precision=HI)
    lower_factor = jnp.linalg.cholesky(gram)
    basis = lax.linalg.triangular_solve(lower_factor, left, left_side=True, lower=True)

    w = lax.dot_general(split3(basis), activations, (((1,), (1,)), ((), ())), preferred_element_type=jnp.float32)
    w = w[:32] + w[32:64] + w[64:]
    w = double(w, cp, PIN)
    w = double(w, cq, QIN)
    w = double(w, hp, POUT)
    w = double(w, hq, QOUT)
    w = w.swapaxes(1, 2).reshape(4, 4, 32, 256)[jnp.array([0, 1, 3, 2])][:, jnp.array([0, 1, 3, 2])]
    w = jnp.where(core == 0, w, w.swapaxes(0, 1))
    w = w.transpose(2, 0, 1, 3).reshape(32, 4096)
    right = exact_dot(w, output_grads, ((1,), (0,)))
    right = right + lax.dot_general(basis, errors, (((1,), (0,)), ((), ())), precision=HI)
    for perm in (CORE, XIN, XOUT):
        right = right + send(right, perm)
    right = right / 8

    grad = lax.dot_general(gathered, output_grads, (((0,), (0,)), ((), ())), preferred_element_type=jnp.float32)
    update = lax.dot_general(basis, right, (((0,), (0,)), ((), ())), precision=HI)
    return ((errors + grad - update)[None], basis.T, right.T)


def solution(mesh):
    placed = (
        P(("replica", "shard"), None),
        P("replica", "shard"),
        P("replica", None, "shard"),
        P("shard", None),
    )
    return jax.shard_map(
        local,
        mesh=mesh,
        in_specs=placed,
        out_specs=(P("replica", None, "shard"), P(), P("shard", None)),
        check_vma=False,
    )
```

time: 488 us -> 259 us (0.53)
  waiting for transfers between devices: 403 us -> 122 us
  starting transfers between devices: 0.3 us -> 44.9 us
  local copies, waits for them, and re-layouts: 0.09 us -> 6.55 us
    psum x2 -> x0, waiting for transfers between devices: 200 us -> none  [the longest x1 145 us: local(): left = lax.psum(partial_value, ('replica', 'shard'))]
    all_gather x1, waiting for transfers between devices: 203 us -> 45 us  [local(): gathered = lax.all_gather(activations, 'shard', axis=0, tiled=True)]
    ppermute x0 -> x21, waiting for transfers between devices: none -> 75.9 us  [send(): return lax.ppermute(a, ALL, perm)]
    ppermute x0 -> x21, starting transfers between devices: none -> 44.8 us  [send(): return lax.ppermute(a, ALL, perm)]
    dot_general x5 -> x9, matrix products: 60 us -> 60.5 us  [the longest x1 22.7 us: local(): lax.dot_general(gathered, output_grads, (((0,), (0,)), ((), ())), preferr...]
  transfers between devices with their start and end apart: 3 -> 22, of which waited for: 3 -> 22; matrix products, arithmetic and copies ran while one was open for 0% -> 17% of each run, Pallas kernels for 0% -> 0%
where the time goes in v1:
time: 259 us
  waiting for transfers between devices  122 us (47%)
  matrix products  61.3 us (24%)
  starting transfers between devices  44.9 us (17%)
  between operations  14.6 us (6%)
  other arithmetic  10.2 us (4%)
  local copies, waits for them, and re-layouts  6.55 us (3%)
    ppermute x21, waiting for transfers between devices, send(): return lax.ppermute(a, ALL, perm)  75.9 us
    all_gather x1, waiting for transfers between devices, local(): gathered = lax.all_gather(activations, 'shard', axis=0, tiled=True)  45 us
    ppermute x21, starting transfers between devices, send(): return lax.ppermute(a, ALL, perm)  44.8 us
    dot_general x1, matrix products, local(): lax.dot_general(gathered, output_grads, (((0,), (0,)), ((), ())), preferr...  22.7 us
    dot_general x1, matrix products, local(): lax.dot_general(basis, right, (((0,), (0,)), ((), ())), precision=HI)  12.2 us
    dot_general x1, matrix products, local(): lax.dot_general(factor_t, errors, (((1,), (1,)), ((), ())), precision=HI)  10.1 us
    dot_general x3, matrix products, exact_dot(): lax.dot_general(split3(a32), b16, (dims, ((), ())), preferred_element_typ...  7.18 us
    dot_general x1, matrix products, local(): lax.dot_general(basis, errors, (((1,), (0,)), ((), ())), precision=HI)  6.68 us
  transfers between devices with their start and end apart: 22, of which 22 were waited for; matrix products, arithmetic and copies ran while one was open for 17% of the time, Pallas kernels for 0%

profile of v1, /device:TPU:1, one launch (start us, length us, event | category | flops | bytes accessed | tf_op | source)
XLA Modules:
  0.0 259.1 jit_solution(10401529710254289043)
XLA Ops:
  8.8 3.6 %fusion.30 = f32[96,4096]{1,0:T(8,128)S(1)} fusion(bf16[4096,512]{1,0:T(8,128)(2,1)} %param.9, bf16[32,512]{1,0:T(8,128)(2,1)S(1)} %get-tuple-element.18, bf16[32,512]{1,0:T(8,128)(2,1)S(1)} %get-tuple-element.19, bf16[32,512]{1,0:T(8,128)(2,1)S(1)} %get-tuple-element.17), kind=kOutput, calls=%fused_computation.68 | convolution fusion | flops 402948096 | bytes 5865472 | tf_op jit(solution)/shard_map/dot_general | solution.py:56
  16.3 3.6 %collective-permute-start = (f32[2,2,2,32,256]{4,3,0,2,1:T(8,128)S(1)}, f32[2,2,2,32,256]{4,3,0,2,1:T(8,128)S(1)}, u32[]{:S(2)}, u32[]{:S(2)}) collective-permute-start(f32[2,2,2,32,256]{4,3,0,2,1:T(8,128)S(1)} %bitcast.159), channel_id=1, source_target_pairs={{0,12},{1,13},{2,14},{3,15},{4,8},{5,9},{6,10},{7,11},{8,4},{9,5},... | collective-permute-start | bytes 786440 | tf_op jit(solution)/shard_map/ppermute | solution.py:45
  19.9 4.1 %collective-permute-done = f32[2,2,2,32,256]{4,3,0,2,1:T(8,128)S(1)} collective-permute-done((f32[2,2,2,32,256]{4,3,0,2,1:T(8,128)S(1)}, f32[2,2,2,32,256]{4,3,0,2,1:T(8,128)S(1)}, u32[]{:S(2)}, u32[]{:S(2)}) %collective-permute-start) | collective-permute-done | bytes 262176 | tf_op jit(solution)/shard_map/ppermute | solution.py:45
  24.1 3.8 %collective-permute-start.1 = (f32[2,2,32,256]{3,2,0,1:T(8,128)S(1)}, f32[2,2,32,256]{3,2,0,1:T(8,128)S(1)}, u32[]{:S(2)}, u32[]{:S(2)}) collective-permute-start(f32[2,2,32,256]{3,2,0,1:T(8,128)S(1)} %select_bitcast_fusion.1), channel_id=1, source_target_pairs={{0,3},{1,2},{2,1},{3,0},{4,7},{5,6},{6,5},{7,4},{8,11},{9,10},{10,... | collective-permute-start | bytes 393224 | tf_op jit(solution)/shard_map/ppermute | solution.py:45
  27.9 4.5 %collective-permute-done.1 = f32[2,2,32,256]{3,2,0,1:T(8,128)S(1)} collective-permute-done((f32[2,2,32,256]{3,2,0,1:T(8,128)S(1)}, f32[2,2,32,256]{3,2,0,1:T(8,128)S(1)}, u32[]{:S(2)}, u32[]{:S(2)}) %collective-permute-start.1) | collective-permute-done | bytes 131104 | tf_op jit(solution)/shard_map/ppermute | solution.py:45
  32.6 4.8 %collective-permute-done.2 = f32[2,32,256]{2,1,0:T(8,128)S(1)} collective-permute-done((f32[2,32,256]{2,1,0:T(8,128)S(1)}, f32[2,32,256]{2,1,0:T(8,128)S(1)}, u32[]{:S(2)}, u32[]{:S(2)}) %collective-permute-start.2) | collective-permute-done | bytes 65568 | tf_op jit(solution)/shard_map/ppermute | solution.py:45
  37.6 3.9 %collective-permute-done.3 = f32[32,256]{1,0:T(8,128)S(1)} collective-permute-done((f32[32,256]{1,0:T(8,128)S(1)}, f32[32,256]{1,0:T(8,128)S(1)}, u32[]{:S(2)}, u32[]{:S(2)}) %collective-permute-start.3) | collective-permute-done | bytes 32800 | tf_op jit(solution)/shard_map/ppermute | solution.py:45
  42.0 10.1 %fusion.6 = f32[32,4096]{1,0:T(8,128)S(1)} fusion(f32[512,32]{0,1:T(8,128)S(1)} %copy-done.2, f32[1,4096,512]{2,1,0:T(8,128)} %param.10, f32[96,4096]{1,0:T(8,128)S(1)} %fusion.40), kind=kOutput, calls=%fused_computation.11 | convolution fusion | flops 805699584 | bytes 10551296 | tf_op jit(solution)/shard_map/dot_general | solution.py:102
  52.6 4.4 %collective-permute-start.4 = (f32[2,2,32,512]{3,2,1,0:T(8,128)S(1)}, f32[2,2,32,512]{3,2,1,0:T(8,128)S(1)}, u32[]{:S(2)}, u32[]{:S(2)}) collective-permute-start(f32[2,2,32,512]{3,2,1,0:T(8,128)S(1)} %bitcast.157), channel_id=1, source_target_pairs={{0,16},{1,17},{2,18},{3,19},{4,20},{5,21},{6,22},{7,23},{8,24},{9,... | collective-permute-start | bytes 786440 | tf_op jit(solution)/shard_map/ppermute | solution.py:45
  60.8 3.5 %collective-permute-done.5 = f32[2,32,512]{2,1,0:T(8,128)S(1)} collective-permute-done((f32[2,32,512]{2,1,0:T(8,128)S(1)}, f32[2,32,512]{2,1,0:T(8,128)S(1)}, u32[]{:S(2)}, u32[]{:S(2)}) %collective-permute-start.5) | collective-permute-done | bytes 131104 | tf_op jit(solution)/shard_map/ppermute | solution.py:45
  77.6 3.4 %collective-permute-done.9 = f32[32,512]{1,0:T(8,128)S(1)} collective-permute-done((f32[32,512]{1,0:T(8,128)S(1)}, f32[32,512]{1,0:T(8,128)S(1)}, u32[]{:S(2)}, u32[]{:S(2)}) %collective-permute-start.9) | collective-permute-done | bytes 65568 | tf_op jit(solution)/shard_map/ppermute | solution.py:45
  81.0 3.8 %collective-permute-start.10 = (f32[32,512]{1,0:T(8,128)S(1)}, f32[32,512]{1,0:T(8,128)S(1)}, u32[]{:S(2)}, u32[]{:S(2)}) collective-permute-start(f32[32,512]{1,0:T(8,128)S(1)} %add.129), channel_id=1, source_target_pairs={{0,12},{1,13},{2,14},{3,15},{4,8},{5,9},{6,10},{7,11},{8,4},{9,5},... | collective-permute-start | bytes 196616 | tf_op jit(solution)/shard_map/ppermute | solution.py:45
  84.8 3.7 %collective-permute-done.10 = f32[32,512]{1,0:T(8,128)S(1)} collective-permute-done((f32[32,512]{1,0:T(8,128)S(1)}, f32[32,512]{1,0:T(8,128)S(1)}, u32[]{:S(2)}, u32[]{:S(2)}) %collective-permute-start.10) | collective-permute-done | bytes 65568 | tf_op jit(solution)/shard_map/ppermute | solution.py:45
  88.6 3.4 %collective-permute-done.11 = f32[32,512]{1,0:T(8,128)S(1)} collective-permute-done((f32[32,512]{1,0:T(8,128)S(1)}, f32[32,512]{1,0:T(8,128)S(1)}, u32[]{:S(2)}, u32[]{:S(2)}) %collective-permute-start.11) | collective-permute-done | bytes 65568 | tf_op jit(solution)/shard_map/ppermute | solution.py:45
  97.9 7.8 %collective-permute-start.13 = (f32[2,2,32,512]{3,1,2,0:T(2,128)S(1)}, f32[2,2,32,512]{3,1,2,0:T(2,128)S(1)}, u32[]{:S(2)}, u32[]{:S(2)}) collective-permute-start(f32[2,2,32,512]{3,1,2,0:T(2,128)S(1)} %maximum_select_fusion.2), channel_id=1, source_target_pairs={{0,16},{1,17},{2,18},{3,19},{4,20},{5,21},{6,22},{7,23},{8,24},{9,... | collective-permute-start | bytes 786440 | tf_op jit(solution)/shard_map/ppermute | solution.py:45
  117.1 3.8 %collective-permute-done.14 = f32[32,256]{1,0:T(8,128)S(1)} collective-permute-done((f32[32,256]{1,0:T(8,128)S(1)}, f32[32,256]{1,0:T(8,128)S(1)}, u32[]{:S(2)}, u32[]{:S(2)}) %collective-permute-start.14) | collective-permute-done | bytes 32800 | tf_op jit(solution)/shard_map/ppermute | solution.py:45
  121.0 4.9 %collective-permute-done.15 = f32[2,32,256]{2,1,0:T(8,128)S(1)} collective-permute-done((f32[2,32,256]{2,1,0:T(8,128)S(1)}, f32[2,32,256]{2,1,0:T(8,128)S(1)}, u32[]{:S(2)}, u32[]{:S(2)}) %collective-permute-start.15) | collective-permute-done | bytes 65568 | tf_op jit(solution)/shard_map/ppermute | solution.py:45
  129.0 5.5 %collective-permute-done.16 = f32[2,2,32,256]{3,2,1,0:T(8,128)S(1)} collective-permute-done((f32[2,2,32,256]{3,2,1,0:T(8,128)S(1)}, f32[2,2,32,256]{3,2,1,0:T(8,128)S(1)}, u32[]{:S(2)}, u32[]{:S(2)}) %collective-permute-start.16) | collective-permute-done | bytes 131104 | tf_op jit(solution)/shard_map/ppermute | solution.py:45
  137.7 9.7 %collective-permute-done.17 = f32[2,2,2,32,256]{4,3,2,1,0:T(8,128)S(1)} collective-permute-done((f32[2,2,2,32,256]{4,3,2,1,0:T(8,128)S(1)}, f32[2,2,2,32,256]{4,3,2,1,0:T(8,128)S(1)}, u32[]{:S(2)}, u32[]{:S(2)}) %collective-permute-start.17) | collective-permute-done | bytes 262176 | tf_op jit(solution)/shard_map/ppermute | solution.py:45
  152.6 6.7 %fusion.9 = f32[32,512]{1,0:T(8,128)S(1)} fusion(f32[32,4096]{1,0:T(8,128)S(1)} %get-tuple-element.22, f32[1,4096,512]{2,1,0:T(8,128)} %param.10, f32[96,512]{1,0:T(8,128)S(1)} %fusion.18), kind=kOutput, calls=%fused_computation.12 | convolution fusion | flops 805355520 | bytes 9175040 | tf_op jit(solution)/shard_map/dot_general | solution.py:128
  163.1 3.5 %collective-permute-done.19 = f32[32,512]{1,0:T(8,128)S(1)} collective-permute-done((f32[32,512]{1,0:T(8,128)S(1)}, f32[32,512]{1,0:T(8,128)S(1)}, u32[]{:S(2)}, u32[]{:S(2)}) %collective-permute-start.19) | collective-permute-done | bytes 65568 | tf_op jit(solution)/shard_map/ppermute | solution.py:45
  172.3 45.0 %all-gather.2.cloned.1.call-done = bf16[4096,4096]{1,0:T(8,128)(2,1)} async-done(((bf16[256,4096]{1,0:T(8,128)(2,1)}), bf16[4096,4096]{1,0:T(8,128)(2,1)}) %all-gather.2.cloned.1.call-update) | async-done | bytes 33554448 | tf_op jit(solution)/shard_map/all_gather | solution.py:89
  217.3 22.7 %fusion.58 = f32[4096,512]{1,0:T(8,128)S(1)} fusion(bf16[4096,4096]{1,0:T(8,128)(2,1)} %all-gather.2.cloned.1.call-done, bf16[4096,512]{1,0:T(8,128)(2,1)} %param.9), kind=kOutput, calls=%fused_computation.124 | convolution fusion | flops 17179869184 | bytes 46137344 | tf_op jit(solution)/shard_map/dot_general | solution.py:133
  240.0 12.2 %fusion.5 = f32[1,4096,512]{2,1,0:T(8,128)} fusion(f32[4096,512]{1,0:T(8,128)S(1)} %fusion.58, f32[1,4096,512]{2,1,0:T(8,128)} %param.10, f32[32,4096]{1,0:T(8,128)S(1)} %get-tuple-element.22, f32[32,512]{1,0:T(8,128)S(1)} %add.140, f32[32,512]{1,0:T(8,128)S(1)} %collective-permute-done.20), kind=kOutput, calls=%fused_computation.10 | convolution fusion | flops 809533440 | bytes 25821184 | tf_op jit(solution)/shard_map/dot_general | solution.py:134
  (108 shorter events, 62.0 us)
Async XLA Ops:
  7.2 210.1 %all-gather.2.cloned.1.call-start = ((), (), s32[]{:S(2)}) async-start(), calls=%async_computation | async-start | bytes 35651584 | tf_op jit(solution)/shard_map/all_gather | solution.py:89
  12.5 29.1 %copy-start = (bf16[256,4096]{1,0:T(8,128)(2,1)S(1)}, bf16[256,4096]{1,0:T(8,128)(2,1)}, u32[]{:S(2)}) copy-start(bf16[256,4096]{1,0:T(8,128)(2,1)} %param.8) | copy-start | bytes 6291460
  16.3 7.7 %collective-permute-start = (f32[2,2,2,32,256]{4,3,0,2,1:T(8,128)S(1)}, f32[2,2,2,32,256]{4,3,0,2,1:T(8,128)S(1)}, u32[]{:S(2)}, u32[]{:S(2)}) collective-permute-start(f32[2,2,2,32,256]{4,3,0,2,1:T(8,128)S(1)} %bitcast.159), channel_id=1, source_target_pairs={{0,12},{1,13},{2,14},{3,15},{4,8},{5,9},{6,10},{7,11},{8,4},{9,5},... | collective-permute-start | bytes 786440 | tf_op jit(solution)/shard_map/ppermute | solution.py:45
  24.1 8.4 %collective-permute-start.1 = (f32[2,2,32,256]{3,2,0,1:T(8,128)S(1)}, f32[2,2,32,256]{3,2,0,1:T(8,128)S(1)}, u32[]{:S(2)}, u32[]{:S(2)}) collective-permute-start(f32[2,2,32,256]{3,2,0,1:T(8,128)S(1)} %select_bitcast_fusion.1), channel_id=1, source_target_pairs={{0,3},{1,2},{2,1},{3,0},{4,7},{5,6},{6,5},{7,4},{8,11},{9,10},{10,... | collective-permute-start | bytes 393224 | tf_op jit(solution)/shard_map/ppermute | solution.py:45
  32.5 5.0 %collective-permute-start.2 = (f32[2,32,256]{2,1,0:T(8,128)S(1)}, f32[2,32,256]{2,1,0:T(8,128)S(1)}, u32[]{:S(2)}, u32[]{:S(2)}) collective-permute-start(f32[2,32,256]{2,1,0:T(8,128)S(1)} %select_bitcast_fusion.3), channel_id=1, source_target_pairs={{0,4},{1,5},{2,6},{3,7},{4,0},{5,1},{6,2},{7,3},{8,12},{9,13},{10,... | collective-permute-start | bytes 196616 | tf_op jit(solution)/shard_map/ppermute | solution.py:45
  37.5 4.0 %collective-permute-start.3 = (f32[32,256]{1,0:T(8,128)S(1)}, f32[32,256]{1,0:T(8,128)S(1)}, u32[]{:S(2)}, u32[]{:S(2)}) collective-permute-start(f32[32,256]{1,0:T(8,128)S(1)} %select_bitcast_fusion.4), channel_id=1, source_target_pairs={{0,1},{1,0},{2,3},{3,2},{4,5},{5,4},{6,7},{7,6},{8,9},{9,8},{10,11... | collective-permute-start | bytes 98312 | tf_op jit(solution)/shard_map/ppermute | solution.py:45
  52.6 5.5 %collective-permute-start.4 = (f32[2,2,32,512]{3,2,1,0:T(8,128)S(1)}, f32[2,2,32,512]{3,2,1,0:T(8,128)S(1)}, u32[]{:S(2)}, u32[]{:S(2)}) collective-permute-start(f32[2,2,32,512]{3,2,1,0:T(8,128)S(1)} %bitcast.157), channel_id=1, source_target_pairs={{0,16},{1,17},{2,18},{3,19},{4,20},{5,21},{6,22},{7,23},{8,24},{9,... | collective-permute-start | bytes 786440 | tf_op jit(solution)/shard_map/ppermute | solution.py:45
  58.2 6.1 %collective-permute-start.5 = (f32[2,32,512]{2,1,0:T(8,128)S(1)}, f32[2,32,512]{2,1,0:T(8,128)S(1)}, u32[]{:S(2)}, u32[]{:S(2)}) collective-permute-start(f32[2,32,512]{2,1,0:T(8,128)S(1)} %select_bitcast_fusion), channel_id=1, source_target_pairs={{0,96},{1,97},{2,98},{3,99},{4,100},{5,101},{6,102},{7,103},{8,104... | collective-permute-start | bytes 393224 | tf_op jit(solution)/shard_map/ppermute | solution.py:45
  64.4 3.2 %collective-permute-start.6 = (f32[32,512]{1,0:T(8,128)S(1)}, f32[32,512]{1,0:T(8,128)S(1)}, u32[]{:S(2)}, u32[]{:S(2)}) collective-permute-start(f32[32,512]{1,0:T(8,128)S(1)} %select_bitcast_fusion.2), channel_id=1, source_target_pairs={{0,32},{1,33},{2,34},{3,35},{4,36},{5,37},{6,38},{7,39},{8,40},{9,... | collective-permute-start | bytes 196616 | tf_op jit(solution)/shard_map/ppermute | solution.py:45
  67.6 3.2 %collective-permute-start.7 = (f32[32,512]{1,0:T(8,128)S(1)}, f32[32,512]{1,0:T(8,128)S(1)}, u32[]{:S(2)}, u32[]{:S(2)}) collective-permute-start(f32[32,512]{1,0:T(8,128)S(1)} %bitcast_add_fusion.3), channel_id=1, source_target_pairs={{0,1},{1,0},{2,3},{3,2},{4,5},{5,4},{6,7},{7,6},{8,9},{9,8},{10,11... | collective-permute-start | bytes 196616 | tf_op jit(solution)/shard_map/ppermute | solution.py:45
  70.8 3.4 %collective-permute-start.8 = (f32[32,512]{1,0:T(8,128)S(1)}, f32[32,512]{1,0:T(8,128)S(1)}, u32[]{:S(2)}, u32[]{:S(2)}) collective-permute-start(f32[32,512]{1,0:T(8,128)S(1)} %add.127), channel_id=1, source_target_pairs={{0,4},{1,5},{2,6},{3,7},{4,0},{5,1},{6,2},{7,3},{8,12},{9,13},{10,... | collective-permute-start | bytes 196616 | tf_op jit(solution)/shard_map/ppermute | solution.py:45
  74.2 6.8 %collective-permute-start.9 = (f32[32,512]{1,0:T(8,128)S(1)}, f32[32,512]{1,0:T(8,128)S(1)}, u32[]{:S(2)}, u32[]{:S(2)}) collective-permute-start(f32[32,512]{1,0:T(8,128)S(1)} %add.128), channel_id=1, source_target_pairs={{0,3},{1,2},{2,1},{3,0},{4,7},{5,6},{6,5},{7,4},{8,11},{9,10},{10,... | collective-permute-start | bytes 196616 | tf_op jit(solution)/shard_map/ppermute | solution.py:45
  81.0 7.4 %collective-permute-start.10 = (f32[32,512]{1,0:T(8,128)S(1)}, f32[32,512]{1,0:T(8,128)S(1)}, u32[]{:S(2)}, u32[]{:S(2)}) collective-permute-start(f32[32,512]{1,0:T(8,128)S(1)} %add.129), channel_id=1, source_target_pairs={{0,12},{1,13},{2,14},{3,15},{4,8},{5,9},{6,10},{7,11},{8,4},{9,5},... | collective-permute-start | bytes 196616 | tf_op jit(solution)/shard_map/ppermute | solution.py:45
  88.5 3.6 %collective-permute-start.11 = (f32[32,512]{1,0:T(8,128)S(1)}, f32[32,512]{1,0:T(8,128)S(1)}, u32[]{:S(2)}, u32[]{:S(2)}) collective-permute-start(f32[32,512]{1,0:T(8,128)S(1)} %add.130), channel_id=1, source_target_pairs={{0,32},{1,33},{2,34},{3,35},{4,36},{5,37},{6,38},{7,39},{8,40},{9,... | collective-permute-start | bytes 196616 | tf_op jit(solution)/shard_map/ppermute | solution.py:45
  92.3 5.5 %collective-permute-start.12 = (f32[2,32,512]{2,0,1:T(2,128)S(1)}, f32[2,32,512]{2,0,1:T(2,128)S(1)}, u32[]{:S(2)}, u32[]{:S(2)}) collective-permute-start(f32[2,32,512]{2,0,1:T(2,128)S(1)} %maximum_select_fusion.6), channel_id=1, source_target_pairs={{0,96},{1,97},{2,98},{3,99},{4,100},{5,101},{6,102},{7,103},{8,104... | collective-permute-start | bytes 393224 | tf_op jit(solution)/shard_map/ppermute | solution.py:45
  97.9 8.9 %collective-permute-start.13 = (f32[2,2,32,512]{3,1,2,0:T(2,128)S(1)}, f32[2,2,32,512]{3,1,2,0:T(2,128)S(1)}, u32[]{:S(2)}, u32[]{:S(2)}) collective-permute-start(f32[2,2,32,512]{3,1,2,0:T(2,128)S(1)} %maximum_select_fusion.2), channel_id=1, source_target_pairs={{0,16},{1,17},{2,18},{3,19},{4,20},{5,21},{6,22},{7,23},{8,24},{9,... | collective-permute-start | bytes 786440 | tf_op jit(solution)/shard_map/ppermute | solution.py:45
  116.2 123.8 %copy-start.1 = (f32[32,4096]{1,0:T(8,128)}, f32[32,4096]{1,0:T(8,128)S(1)}, u32[]{:S(2)}) copy-start(f32[32,4096]{1,0:T(8,128)S(1)} %get-tuple-element.22) | copy-start | bytes 1572868
  117.0 3.9 %collective-permute-start.14 = (f32[32,256]{1,0:T(8,128)S(1)}, f32[32,256]{1,0:T(8,128)S(1)}, u32[]{:S(2)}, u32[]{:S(2)}) collective-permute-start(f32[32,256]{1,0:T(8,128)S(1)} %slice_add_fusion.6), channel_id=1, source_target_pairs={{0,1},{1,0},{2,3},{3,2},{4,5},{5,4},{6,7},{7,6},{8,9},{9,8},{10,11... | collective-permute-start | bytes 98312 | tf_op jit(solution)/shard_map/ppermute | solution.py:45
  120.9 5.0 %collective-permute-start.15 = (f32[2,32,256]{2,1,0:T(8,128)S(1)}, f32[2,32,256]{2,1,0:T(8,128)S(1)}, u32[]{:S(2)}, u32[]{:S(2)}) collective-permute-start(f32[2,32,256]{2,1,0:T(8,128)S(1)} %maximum_select_fusion.9), channel_id=1, source_target_pairs={{0,4},{1,5},{2,6},{3,7},{4,0},{5,1},{6,2},{7,3},{8,12},{9,13},{10,... | collective-permute-start | bytes 196616 | tf_op jit(solution)/shard_map/ppermute | solution.py:45
  125.9 8.6 %collective-permute-start.16 = (f32[2,2,32,256]{3,2,1,0:T(8,128)S(1)}, f32[2,2,32,256]{3,2,1,0:T(8,128)S(1)}, u32[]{:S(2)}, u32[]{:S(2)}) collective-permute-start(f32[2,2,32,256]{3,2,1,0:T(8,128)S(1)} %maximum_select_fusion.7), channel_id=1, source_target_pairs={{0,3},{1,2},{2,1},{3,0},{4,7},{5,6},{6,5},{7,4},{8,11},{9,10},{10,... | collective-permute-start | bytes 393224 | tf_op jit(solution)/shard_map/ppermute | solution.py:45
  134.5 12.9 %collective-permute-start.17 = (f32[2,2,2,32,256]{4,3,2,1,0:T(8,128)S(1)}, f32[2,2,2,32,256]{4,3,2,1,0:T(8,128)S(1)}, u32[]{:S(2)}, u32[]{:S(2)}) collective-permute-start(f32[2,2,2,32,256]{4,3,2,1,0:T(8,128)S(1)} %maximum_select_fusion.4), channel_id=1, source_target_pairs={{0,12},{1,13},{2,14},{3,15},{4,8},{5,9},{6,10},{7,11},{8,4},{9,5},... | collective-permute-start | bytes 786440 | tf_op jit(solution)/shard_map/ppermute | solution.py:45
  159.3 3.8 %collective-permute-start.18 = (f32[32,512]{1,0:T(8,128)S(1)}, f32[32,512]{1,0:T(8,128)S(1)}, u32[]{:S(2)}, u32[]{:S(2)}) collective-permute-start(f32[32,512]{1,0:T(8,128)S(1)} %fusion.9), channel_id=1, source_target_pairs={{0,16},{1,17},{2,18},{3,19},{4,20},{5,21},{6,22},{7,23},{8,24},{9,... | collective-permute-start | bytes 196616 | tf_op jit(solution)/shard_map/ppermute | solution.py:45
  163.0 3.6 %collective-permute-start.19 = (f32[32,512]{1,0:T(8,128)S(1)}, f32[32,512]{1,0:T(8,128)S(1)}, u32[]{:S(2)}, u32[]{:S(2)}) collective-permute-start(f32[32,512]{1,0:T(8,128)S(1)} %add.139), channel_id=1, source_target_pairs={{0,32},{1,33},{2,34},{3,35},{4,36},{5,37},{6,38},{7,39},{8,40},{9,... | collective-permute-start | bytes 196616 | tf_op jit(solution)/shard_map/ppermute | solution.py:45
  166.6 5.0 %collective-permute-start.20 = (f32[32,512]{1,0:T(8,128)S(1)}, f32[32,512]{1,0:T(8,128)S(1)}, u32[]{:S(2)}, u32[]{:S(2)}) collective-permute-start(f32[32,512]{1,0:T(8,128)S(1)} %add.140), channel_id=1, source_target_pairs={{0,96},{1,97},{2,98},{3,99},{4,100},{5,101},{6,102},{7,103},{8,104... | collective-permute-start | bytes 196616 | tf_op jit(solution)/shard_map/ppermute | solution.py:45
  (2 other events, 31.5 us)
Sparse Core Ops, SparseCore 0:
  10.1 207.0 all-gather.1

commit v2 on v0

v2 whole, which is shorter than its diff:
```python
import functools

import jax
import jax.numpy as jnp
from jax import lax
from jax.experimental import pallas as pl
from jax.experimental.pallas import tpu as pltpu
from jax.sharding import PartitionSpec as P

ALL = ("replica", "shard")
NX, NC, NZ, NY = 4, 2, 4, 4
RANK = 32
UNIT = 256
PART = 2048
WIDTH = 512
STRIP = 512
F32, BF16 = jnp.float32, jnp.bfloat16
NN, NT, TN = (((1,), (0,)), ((), ())), (((1,), (1,)), ((), ())), (((0,), (0,)), ((), ()))


def pairs(move):
    out = []
    for x in range(NX):
        for c in range(NC):
            for z in range(NZ):
                for y in range(NY):
                    a, b, d, e = move(x, c, z, y)
                    out.append((((x * NC + c) * NZ + z) * NY + y, ((a * NC + b) * NZ + d) * NY + e))
    return out


def inner(v):
    return v ^ 1


def outer(v):
    return 3 - v


def on_p(f):
    return pairs(lambda x, c, z, y: (x, c, z, f(y)) if c == 0 else (x, c, f(z), y))


def on_q(f):
    return pairs(lambda x, c, z, y: (x, c, f(z), y) if c == 0 else (x, c, z, f(y)))


def up(v):
    return (v + 1) % 4


def down(v):
    return (v + 3) % 4


PIN, POUT, QIN, QOUT = on_p(inner), on_p(outer), on_q(inner), on_q(outer)
PUP, PDOWN, QUP, QDOWN = on_p(up), on_p(down), on_q(up), on_q(down)
XIN = pairs(lambda x, c, z, y: (inner(x), c, z, y))
XOUT = pairs(lambda x, c, z, y: (outer(x), c, z, y))
CORE = pairs(lambda x, c, z, y: (x, 1 - c, z, y))


def dot(a, b, dims):
    return lax.dot_general(a, b, dims, preferred_element_type=F32)


def split(a):
    hi = a.astype(BF16)
    rest = a - hi.astype(F32)
    mid = rest.astype(BF16)
    return hi, mid, (rest - mid.astype(F32)).astype(BF16)


def fold(a):
    return a[:RANK] + a[RANK : 2 * RANK] + a[2 * RANK :]


def wide_dot(three, b, dims):
    hi, mid, lo = split(b)
    d = dot(three[: 2 * RANK], mid, dims)
    return fold(dot(three, hi, dims)) + (d[:RANK] + d[RANK:]) + dot(three[:RANK], lo, dims)


def kernel_call(
    body, name, grid, in_specs, out_specs, out_shape, scratch=(), prefetch=0, aliases=None, vmem=16, us=3, after=()
):
    first = prefetch + len(in_specs)

    def run(*refs):
        body(*refs[:first], *refs[first + len(after) :])

    call = pl.pallas_call(
        run,
        grid_spec=pltpu.PrefetchScalarGridSpec(
            num_scalar_prefetch=prefetch,
            grid=grid,
            in_specs=in_specs + [pl.BlockSpec(memory_space=pl.ANY)] * len(after),
            out_specs=out_specs,
            scratch_shapes=list(scratch),
        ),
        out_shape=out_shape,
        input_output_aliases=aliases or {},
        compiler_params=pltpu.CompilerParams(vmem_limit_bytes=vmem * 2**20),
        cost_estimate=pl.CostEstimate(flops=0, bytes_accessed=0, transcendentals=0),
        name=name,
    )
    return lambda *args: call(*args, *after)


def shape(*dims, dtype=F32):
    return jax.ShapeDtypeStruct(dims, dtype)


def turn_kernel(acts, unit0, unit1):
    half = PART // 512
    for dst, inside in ((unit0, pl.program_id(0) < half), (unit1, pl.program_id(0) >= half)):

        @pl.when(inside)
        def _(dst=dst):
            dst[...] = acts[...].T


def turn(acts):
    half = PART // 512
    return kernel_call(
        turn_kernel,
        "turn",
        (2 * half,),
        [pl.BlockSpec((UNIT, 512), lambda i: (0, i))],
        [
            pl.BlockSpec((512, UNIT), lambda i: (jnp.minimum(i, half - 1), 0)),
            pl.BlockSpec((512, UNIT), lambda i: (jnp.maximum(i - half, 0), 0)),
        ],
        [shape(PART, UNIT, dtype=BF16)] * 2,
    )(acts)


def line_kernel(*refs):
    for k, ref in enumerate(refs[:4]):
        refs[-1][:, k * UNIT : (k + 1) * UNIT] = ref[...]


def join_line(units, *after):
    return kernel_call(
        line_kernel,
        "line",
        (PART // 512,),
        [pl.BlockSpec((512, UNIT), lambda i: (i, 0))] * 4,
        pl.BlockSpec((512, 4 * UNIT), lambda i: (i, 0)),
        shape(PART, 4 * UNIT, dtype=BF16),
        after=after,
    )(*units)


def arrange_kernel(order, g0, g1, g2, g3, out):
    for k, g in enumerate((g0, g1, g2, g3)):
        out[k * UNIT : (k + 1) * UNIT, :] = g[...]


def arrange(order, grads):
    def block(t):
        return pl.BlockSpec((UNIT, WIDTH), lambda m, o: (o[4 * m + t], 0))

    return kernel_call(
        arrange_kernel,
        "arrange",
        (4,),
        [block(t) for t in range(4)],
        pl.BlockSpec((4 * UNIT, WIDTH), lambda m, o: (m, 0)),
        shape(*grads.shape, dtype=BF16),
        prefetch=1,
    )(order, *([grads] * 4))


def tokens_kernel(order, factor, g0, g1, g2, g3, out, three):
    @pl.when(pl.program_id(0) == 0)
    def _():
        three[...] = jnp.concatenate(split(factor[...]), 0)

    for i, g in enumerate((g0, g1, g2, g3)):
        out[i] = fold(dot(three[...], g[...], NT))


def tokens(order, factor, grads):
    def block(t):
        return pl.BlockSpec((UNIT, WIDTH), lambda m, o: (o[4 * m + t], 0))

    return kernel_call(
        tokens_kernel,
        "tokens",
        (4,),
        [pl.BlockSpec((RANK, WIDTH), lambda m, o: (0, 0))] + [block(t) for t in range(4)],
        pl.BlockSpec((4, RANK, UNIT), lambda m, o: (m, 0, 0)),
        shape(16, RANK, UNIT),
        [pltpu.VMEM((3 * RANK, WIDTH), BF16)],
        prefetch=1,
    )(order, factor, *([grads] * 4))


def errors_left_kernel(order, factor, err, out, three):
    @pl.when(pl.program_id(0) == 0)
    def _():
        three[...] = jnp.concatenate(split(factor[...]), 0)

    out[0] = wide_dot(three[...], err[...], NT)


def errors_left(order, factor, errors, *after):
    return kernel_call(
        errors_left_kernel,
        "errors_left",
        (8,),
        [
            pl.BlockSpec((RANK, WIDTH), lambda m, o: (0, 0)),
            pl.BlockSpec((512, WIDTH), lambda m, o: (o[m], 0)),
        ],
        pl.BlockSpec((1, RANK, 512), lambda m, o: (m, 0, 0)),
        shape(8, RANK, 512),
        [pltpu.VMEM((3 * RANK, WIDTH), BF16)],
        prefetch=1,
        vmem=56,
        us=9,
        after=after,
    )(order, factor, errors)


def left_kernel(order, u, part, acts, out):
    three = jnp.concatenate(split(u[...]), 0)
    out[0] = part[0] + fold(dot(three, acts[...], NN))


def left_terms(order, u, part, acts):
    return kernel_call(
        left_kernel,
        "left_terms",
        (8,),
        [
            pl.BlockSpec((RANK, UNIT), lambda m, o: (0, 0)),
            pl.BlockSpec((1, RANK, 512), lambda m, o: (m, 0, 0)),
            pl.BlockSpec((UNIT, 512), lambda m, o: (0, o[m])),
        ],
        pl.BlockSpec((1, RANK, 512), lambda m, o: (m, 0, 0)),
        shape(8, RANK, 512),
        prefetch=1,
    )(order, u, part, acts)


def basis_kernel(order, left, basis, six, inv, work):
    gram = None
    for k in range(8):
        g = lax.dot_general(left[k], left[k], NT, precision=lax.Precision.HIGHEST, preferred_element_type=F32)
        gram = g if gram is None else gram + g
    rows = lax.broadcasted_iota(jnp.int32, (RANK, RANK), 0)
    cols = lax.broadcasted_iota(jnp.int32, (RANK, RANK), 1)
    eye = jnp.where(rows == cols, 1.0, 0.0).astype(F32)
    work[...] = jnp.zeros_like(work)
    work[:, :RANK] = gram
    work[:, RANK : 2 * RANK] = eye
    lane = lax.broadcasted_iota(jnp.int32, (RANK, 128), 1)
    sub = lax.broadcasted_iota(jnp.int32, (RANK, 128), 0)

    a = work[...]
    for j in range(RANK):
        col = jnp.sum(jnp.where(lane == j, a, 0.0), axis=1, keepdims=True)
        row = a[j : j + 1, :]
        pivot = col[j : j + 1, :]
        root = lax.rsqrt(pivot)
        root = root * (1.5 - 0.5 * pivot * root * root)
        scaled = row * root
        factor = jnp.where(sub[:, :1] > j, col * root, 0.0)
        a = jnp.where(sub == j, scaled, a - factor * scaled)
    inverse = a[:, RANK : 2 * RANK]
    inv[...] = inverse
    for k in range(8):
        b = lax.dot_general(inverse, left[k], NN, precision=lax.Precision.HIGHEST, preferred_element_type=F32)
        hi, mid, lo = split(b)
        at = pl.ds(pl.multiple_of(order[k] * 512, 512), 512)
        basis[:, at] = b
        six[at, :] = jnp.concatenate([hi, mid, lo, hi, hi, mid], 0).T


def make_basis(order, left):
    return kernel_call(
        basis_kernel,
        "basis",
        (1,),
        [pl.BlockSpec((8, RANK, 512), lambda m, o: (0, 0, 0))],
        [pl.BlockSpec((RANK, 4096), lambda m, o: (0, 0)), pl.BlockSpec((4096, 6 * RANK), lambda m, o: (0, 0)), pl.BlockSpec((RANK, RANK), lambda m, o: (0, 0))],
        [shape(RANK, 4096), shape(4096, 6 * RANK, dtype=BF16), shape(RANK, RANK)],
        [pltpu.VMEM((RANK, 128), F32)],
        prefetch=1,
    )(order, left)


def project_kernel(order, left, acts, out, total):
    m = pl.program_id(0)
    d = dot(jnp.concatenate(split(left[0]), 0), acts[...], NT)

    @pl.when(m == 0)
    def _():
        total[...] = d

    @pl.when(m > 0)
    def _():
        total[...] += d

    out[...] = fold(total[...])


def project(order, left, acts, *after):
    return kernel_call(
        project_kernel,
        "project",
        (8,),
        [pl.BlockSpec((1, RANK, 512), lambda m, o: (m, 0, 0)), pl.BlockSpec((UNIT, 512), lambda m, o: (0, o[m]))],
        pl.BlockSpec((RANK, UNIT), lambda m, o: (0, 0)),
        shape(RANK, UNIT),
        [pltpu.VMEM((3 * RANK, UNIT), F32)],
        prefetch=1,
        after=after,
    )(order, left, acts)


def errors_right_kernel(order, left, err, out):
    d = wide_dot(jnp.concatenate(split(left[0]), 0), err[...], NN)

    @pl.when(pl.program_id(0) == 0)
    def _():
        out[...] = d

    @pl.when(pl.program_id(0) > 0)
    def _():
        out[...] += d


def errors_right(order, left, errors):
    return kernel_call(
        errors_right_kernel,
        "errors_right",
        (8,),
        [pl.BlockSpec((1, RANK, 512), lambda m, o: (m, 0, 0)), pl.BlockSpec((512, WIDTH), lambda m, o: (o[m], 0))],
        pl.BlockSpec((RANK, WIDTH), lambda m, o: (0, 0)),
        shape(RANK, WIDTH),
        prefetch=1,
    )(order, left, errors)


def right_kernel(order, w, part, inverse, g0, g1, g2, g3, out, total):
    m = pl.program_id(0)
    three = jnp.concatenate([jnp.concatenate(v, 0) for v in (split(w[i]) for i in range(4))], 1)
    d = fold(dot(three, jnp.concatenate([g0[...], g1[...], g2[...], g3[...]], 0), NN))

    @pl.when(m == 0)
    def _():
        total[...] = part[...] + d

    @pl.when(m > 0)
    def _():
        total[...] += d

    @pl.when(m == 3)
    def _():
        out[...] = (
            lax.dot_general(
                inverse[...], total[...], NN, precision=lax.Precision.HIGHEST, preferred_element_type=F32
            )
            / 8.0
        )


def right_terms(order, w, part, inverse, grads, *after):
    def block(t):
        return pl.BlockSpec((UNIT, WIDTH), lambda m, o: (o[4 * m + t], 0))

    return kernel_call(
        right_kernel,
        "right_terms",
        (4,),
        [
            pl.BlockSpec((4, RANK, UNIT), lambda m, o: (m, 0, 0)),
            pl.BlockSpec((RANK, WIDTH), lambda m, o: (0, 0)),
            pl.BlockSpec((RANK, RANK), lambda m, o: (0, 0)),
        ]
        + [block(t) for t in range(4)],
        pl.BlockSpec((RANK, WIDTH), lambda m, o: (0, 0)),
        shape(RANK, WIDTH),
        [pltpu.VMEM((RANK, WIDTH), F32)],
        prefetch=1,
        us=40,
        after=after,
    )(order, w, part, inverse, *([grads] * 4))


def rows_kernel(count, updated, base, *refs):
    out = refs[-1]
    total = base[...]
    for x, g in zip(refs[:count], refs[count : 2 * count]):
        total = total + dot(x[...], g[...], NN)
    if updated:
        six, right = refs[2 * count : 2 * count + 2]
        hi, mid, lo = split(right[...])
        total = total - dot(six[...], jnp.concatenate([hi, hi, hi, mid, lo, mid], 0), NN)
    out[...] = total


def add_rows(base, first, pieces, grads, start, of, update=None, buffer=None):
    count = len(pieces)
    depth = pieces[0][0].shape[1]
    write = start // STRIP
    args = [base] + [x for x, _ in pieces] + [grads] * count
    specs = [pl.BlockSpec((STRIP, WIDTH), lambda i: (first + i, 0))]
    specs += [pl.BlockSpec((STRIP, depth), lambda i: (i, 0))] * count
    specs += [pl.BlockSpec((depth, WIDTH), lambda i, t=t: (t, 0)) for _, t in pieces]
    if update is not None:
        args += update
        specs += [
            pl.BlockSpec((STRIP, 6 * RANK), lambda i: (write + i, 0)),
            pl.BlockSpec((RANK, WIDTH), lambda i: (0, 0)),
        ]
    aliases = None
    if buffer is not None:
        aliases = {len(args): 0}
        args.append(buffer)
        specs.append(pl.BlockSpec(memory_space=pl.ANY))
    return kernel_call(
        functools.partial(rows_kernel, count, update is not None),
        "add_rows",
        (PART // STRIP,),
        specs,
        pl.BlockSpec((STRIP, WIDTH), lambda i: (write + i, 0)),
        shape(of, WIDTH),
        aliases=aliases,
        vmem=36,
    )(*args)


def tie_kernel(*refs):
    pass


def tie(a, *after):
    anywhere = pl.BlockSpec(memory_space=pl.ANY)
    return pl.pallas_call(
        tie_kernel,
        in_specs=[anywhere] * (1 + len(after)),
        out_specs=anywhere,
        out_shape=jax.ShapeDtypeStruct(a.shape, a.dtype),
        input_output_aliases={0: 0},
        name="tie",
    )(a, *after)


def pair_kernel(a, b, *rest):
    n = a.shape[0]
    rest[-1][:n] = a[...]
    rest[-1][n:] = b[...]


def pair(a, b, *others):
    return pl.pallas_call(
        pair_kernel,
        out_shape=jax.ShapeDtypeStruct((2 * a.shape[0],) + a.shape[1:], a.dtype),
        compiler_params=pltpu.CompilerParams(vmem_limit_bytes=16 * 2**20),
        name="pair",
    )(a, b, *others)


def send(a, perm):
    return lax.ppermute(a, ALL, perm)


def local(activations, output_grads, error_buffer, previous_factor):
    errors = error_buffer[0]
    rep, sh = lax.axis_index("replica"), lax.axis_index("shard")
    x, core = rep // 2, rep % 2
    z, y = sh // 4, sh % 4
    p = jnp.where(core == 0, y, z)
    q = jnp.where(core == 0, z, y)
    def shard_of(a, b):
        return jnp.where(core == 0, b * 4 + a, a * 4 + b)

    def int_array(v):
        return jnp.stack(v).astype(jnp.int32)

    def codes(v):
        return [v, v ^ 1, 3 - v, (3 - v) ^ 1]

    def ring(v):
        return [v, (v + 3) % 4, (v + 1) % 4, (v + 2) % 4]

    by_code_q = int_array([shard_of(a, b) for b in codes(q) for a in codes(p)])
    by_code = int_array([shard_of(a, b) for a in codes(p) for b in codes(q)])
    by_ring = int_array([shard_of(a, b) for b in ring(q) for a in ring(p)])
    by_rep = int_array([v * 2 + c for c in (core, 1 - core) for b in (x, 3 - x) for v in (b, b ^ 1)])

    def cat(*a, axis=0):
        return jnp.concatenate(a, axis)

    def place(v, origin):
        d = (v - origin) % 4
        return jnp.where(d == 0, 0, jnp.where(d == 3, 1, d + 1))

    in_kept = int_array([4 * place(b, q) + place(a, p) for a in codes(p) for b in codes(q)])
    factor = previous_factor.T
    units = turn(activations)
    above0, below0 = send(units[0], PUP), send(units[0], PDOWN)
    far0, below1 = send(above0, PUP), send(units[1], PDOWN)
    above1, far1 = send(units[1], PUP), send(below1, PDOWN)

    u = tokens(by_code_q, factor, output_grads)
    u = u[:8] + send(u[8:], QOUT)
    u = u[:4] + send(u[4:], QIN)
    u = send(u, CORE)
    u = u[:2] + send(u[2:], QOUT)
    u = u[0] + send(u[1], QIN)
    line0 = join_line((units[0], above0, below0, far0), u)
    top0, bottom0 = send(line0, QUP), send(line0, QDOWN)
    u = send(u, CORE)
    part = errors_left(by_rep, factor, errors, far0)
    left = left_terms(by_rep, u, part, activations)
    left = left[:4] + send(left[4:], CORE)
    left = left[:2] + send(left[2:], XOUT)
    left = left[0] + send(left[1], XIN)
    line1 = join_line((units[1], above1, below1, far1), left)
    top1, bottom1 = send(line1, QUP), send(line1, QDOWN)
    left = left + send(left, PIN)
    left = left + send(left, POUT)
    left = send(left, CORE)
    top0 = tie(top0, left)
    opposite0 = send(top0, QUP)
    left = left + send(left, PIN)
    left = left + send(left, POUT)
    left = left[None]
    left = cat(left, send(left, XIN))
    left = cat(left, send(left, XOUT))
    left = cat(send(left, CORE), left)

    basis, six, inverse = make_basis(by_rep, left)
    part = errors_right(by_rep, left, errors)
    kept = arrange(by_ring, output_grads)
    w = project(by_rep, left, activations, top0, bottom0)[None]
    w = send(w, CORE)
    w = cat(w, send(w, PIN))
    w = pair(w, send(w, POUT), inverse)
    w = send(w, CORE)
    bottom1 = tie(bottom1, w)
    opposite1 = send(bottom1, QDOWN)
    w = pair(w, send(w, PIN), part)
    w = cat(w, send(w, POUT))
    right = right_terms(in_kept, w, part, inverse, kept, opposite0, bottom1)
    for perm in (CORE, XIN, XOUT):
        right = right + send(right, perm)
    update = (six, right)
    sum1 = add_rows(errors, PART // STRIP, ((line1, 0), (bottom1, 2)), kept, 0, PART)
    blocks = ((line0, 0), (top0, 1), (bottom0, 2), (opposite0, 3))
    out = add_rows(errors, 0, blocks, kept, 0, 2 * PART, update)
    out = add_rows(sum1, 0, ((top1, 1), (opposite1, 3)), kept, PART, 2 * PART, update, out)
    return (out[None], basis.T, right.T)


def solution(mesh):
    placed = (
        P(("replica", "shard"), None),
        P("replica", "shard"),
        P("replica", None, "shard"),
        P("shard", None),
    )
    return jax.shard_map(
        local,
        mesh=mesh,
        in_specs=placed,
        out_specs=(P("replica", None, "shard"), P(), P("shard", None)),
        check_vma=False,
    )
```

time: 488 us -> 235 us (0.48)
  waiting for transfers between devices: 403 us -> 79.2 us
  Pallas kernels: 0 us -> 75.5 us
  matrix products: 61.7 us -> 0 us
  starting transfers between devices: 0.3 us -> 59.1 us
  local copies, waits for them, and re-layouts: 0.09 us -> 18.6 us
  between operations: 13.8 us -> 1.02 us
  other arithmetic: 7.53 us -> 0.31 us
    all_gather x1 -> x0, waiting for transfers between devices: 203 us -> none  [local(): lax.all_gather(activations, 'shard', axis=0, tiled=True)]
    psum x2 -> x0, waiting for transfers between devices: 200 us -> none  [the longest x1 145 us: local(): left = lax.psum(partial_value, ('replica', 'shard'))]
    ppermute x0 -> x38, waiting for transfers between devices: none -> 79.2 us  [send(): return lax.ppermute(a, ALL, perm)]
    pallas_call x0 -> x18, Pallas kernels: none -> 75.5 us  [the longest x14 75.5 us: kernel_call(): return lambda *args: call(*args, *after)]
    dot_general x5 -> x0, matrix products: 60 us -> none  [the longest x1 28 us: local(): lax.dot_general(lax.all_gather(activations, 'shard', axis=0, tiled=True),...]
    ppermute x0 -> x38, starting transfers between devices: none -> 59.1 us  [send(): return lax.ppermute(a, ALL, perm)]
    unnamed x6 -> x39, local copies, waits for them, and re-layouts: 0.02 us -> 17.6 us
    another operation x5 -> x0, other arithmetic: 6.68 us -> none  [the longest x3 3.6 us: local(): lower_factor = jnp.linalg.cholesky(gram)]
  transfers between devices with their start and end apart: 3 -> 38, of which waited for: 3 -> 23; matrix products, arithmetic and copies ran while one was open for 0% -> 1% of each run, Pallas kernels for 0% -> 27%
where the time goes in v2:
time: 235 us; the launch traced here: 234 us
  waiting for transfers between devices  79.2 us (34%)
  Pallas kernels  75.5 us (32%)
  starting transfers between devices  59.1 us (25%)
  local copies, waits for them, and re-layouts  18.6 us (8%)
    ppermute x38, waiting for transfers between devices, send(): return lax.ppermute(a, ALL, perm)  79.2 us
    pallas_call x14, Pallas kernels, kernel_call(): return lambda *args: call(*args, *after)  75.5 us
    ppermute x38, starting transfers between devices, send(): return lax.ppermute(a, ALL, perm)  59.1 us
    unnamed x39, local copies, waits for them, and re-layouts  17.6 us
  transfers between devices with their start and end apart: 38, of which 23 were waited for; matrix products, arithmetic and copies ran while one was open for 1% of the time, Pallas kernels for 27%

profile of v2, /device:TPU:1, one launch (start us, length us, event | category | flops | bytes accessed | tf_op | source)
XLA Modules:
  0.0 233.8 jit_solution(1692093926123135800)
XLA Ops:
  2.2 3.7 %turn.1 = (bf16[2048,256]{1,0:T(8,128)(2,1)}, bf16[2048,256]{1,0:T(8,128)(2,1)}) custom-call(bf16[256,4096]{1,0:T(8,128)(2,1)S(1)} %copy-done.6), custom_call_target="tpu_custom_call" | custom-call | tf_op jit(solution)/shard_map/turn/pallas_call | solution.py:107
  16.7 6.9 %collective-permute-done.3 = f32[8,32,256]{2,1,0:T(8,128)S(1)} collective-permute-done((f32[8,32,256]{2,1,0:T(8,128)S(1)}, f32[8,32,256]{2,1,0:T(8,128)S(1)}, u32[]{:S(2)}, u32[]{:S(2)}) %collective-permute-start.3) | collective-permute-done | bytes 262176 | tf_op jit(solution)/shard_map/ppermute | solution.py:469
  27.6 3.4 %collective-permute-start.5 = (f32[4,32,256]{2,1,0:T(8,128)S(1)}, f32[4,32,256]{2,1,0:T(8,128)S(1)}, u32[]{:S(2)}, u32[]{:S(2)}) collective-permute-start(f32[4,32,256]{2,1,0:T(8,128)S(1)} %slice_add_fusion.3), channel_id=1, source_target_pairs={{0,16},{1,17},{2,18},{3,19},{4,20},{5,21},{6,22},{7,23},{8,24},{9,... | collective-permute-start | bytes 393224 | tf_op jit(solution)/shard_map/ppermute | solution.py:469
  37.6 3.6 %collective-permute-done.7 = f32[32,256]{1,0:T(8,128)S(1)} collective-permute-done((f32[32,256]{1,0:T(8,128)S(1)}, f32[32,256]{1,0:T(8,128)S(1)}, u32[]{:S(2)}, u32[]{:S(2)}) %collective-permute-start.7) | collective-permute-done | bytes 32800 | tf_op jit(solution)/shard_map/ppermute | solution.py:469
  44.8 9.7 %errors_left.1.refs_2_ = f32[8,32,512]{2,1,0:T(8,128)} custom-call(s32[8]{0:T(128)} %stack.184.refs_0_, f32[32,512]{1,0:T(8,128)} %bitcast.79, f32[4096,512]{1,0:T(8,128)} %bitcast.74, bf16[2048,256]{1,0:T(8,128)(2,1)} %copy-done.8), custom_call_target="tpu_custom_call" | custom-call | tf_op jit(solution)/shard_map/errors_left/pallas_call | solution.py:107
  63.6 4.4 %line.3.refs_1_ = bf16[2048,1024]{1,0:T(8,128)(2,1)} custom-call(bf16[2048,256]{1,0:T(8,128)(2,1)} %get-tuple-element.9.refs_0_, bf16[2048,256]{1,0:T(8,128)(2,1)S(1)} %copy-done.12, bf16[2048,256]{1,0:T(8,128)(2,1)} %collective-permute-done.23.refs_2_, bf16[2048,256]{1,0:T(8,128)(2,1)S(1)} %copy-done.9, f32[32,256]{1,0:T(8,128)S(1)} %fusion.1.refs_4_), custom_call_target="tpu_custom_call" | custom-call | tf_op jit(solution)/shard_map/line/pallas_call | solution.py:107
  70.9 3.5 %collective-permute-done.13 = f32[32,512]{1,0:T(8,128)S(1)} collective-permute-done((f32[32,512]{1,0:T(8,128)S(1)}, f32[32,512]{1,0:T(8,128)S(1)}, u32[]{:S(2)}, u32[]{:S(2)}) %collective-permute-start.13) | collective-permute-done | bytes 65568 | tf_op jit(solution)/shard_map/ppermute | solution.py:469
  74.4 4.4 %line.2.refs_1_ = bf16[2048,1024]{1,0:T(8,128)(2,1)} custom-call(bf16[2048,256]{1,0:T(8,128)(2,1)} %get-tuple-element.8.refs_0_, bf16[2048,256]{1,0:T(8,128)(2,1)S(1)} %collective-permute-done.refs_1_, bf16[2048,256]{1,0:T(8,128)(2,1)} %collective-permute-done.1.refs_2_, bf16[2048,256]{1,0:T(8,128)(2,1)S(1)} %collective-permute-done.2.refs_3_, ...), custom_call_target="tpu_custom_call" | custom-call | tf_op jit(solution)/shard_map/line/pallas_call | solution.py:107
  80.1 4.3 %collective-permute-done.15 = f32[32,512]{1,0:T(8,128)S(1)} collective-permute-done((f32[32,512]{1,0:T(8,128)S(1)}, f32[32,512]{1,0:T(8,128)S(1)}, u32[]{:S(2)}, u32[]{:S(2)}) %collective-permute-start.15) | collective-permute-done | bytes 65568 | tf_op jit(solution)/shard_map/ppermute | solution.py:469
  86.9 3.1 %collective-permute-done.16 = f32[32,512]{1,0:T(8,128)S(1)} collective-permute-done((f32[32,512]{1,0:T(8,128)S(1)}, f32[32,512]{1,0:T(8,128)S(1)}, u32[]{:S(2)}, u32[]{:S(2)}) %collective-permute-start.16) | collective-permute-done | bytes 65568 | tf_op jit(solution)/shard_map/ppermute | solution.py:469
  90.0 6.9 %collective-permute-start.17 = (f32[32,512]{1,0:T(8,128)S(1)}, f32[32,512]{1,0:T(8,128)S(1)}, u32[]{:S(2)}, u32[]{:S(2)}) collective-permute-start(f32[32,512]{1,0:T(8,128)S(1)} %add.489), channel_id=1, source_target_pairs={{0,16},{1,17},{2,18},{3,19},{4,20},{5,21},{6,22},{7,23},{8,24},{9,... | collective-permute-start | bytes 196616 | tf_op jit(solution)/shard_map/ppermute | solution.py:469
  97.8 4.3 %collective-permute-done.18 = f32[32,512]{1,0:T(8,128)S(1)} collective-permute-done((f32[32,512]{1,0:T(8,128)S(1)}, f32[32,512]{1,0:T(8,128)S(1)}, u32[]{:S(2)}, u32[]{:S(2)}) %collective-permute-start.18) | collective-permute-done | bytes 65568 | tf_op jit(solution)/shard_map/ppermute | solution.py:469
  102.3 5.4 %collective-permute-done.19 = f32[32,512]{1,0:T(8,128)S(1)} collective-permute-done((f32[32,512]{1,0:T(8,128)S(1)}, f32[32,512]{1,0:T(8,128)S(1)}, u32[]{:S(2)}, u32[]{:S(2)}) %collective-permute-start.19) | collective-permute-done | bytes 65568 | tf_op jit(solution)/shard_map/ppermute | solution.py:469
  112.3 3.8 %collective-permute-start.21 = (f32[2,32,512]{2,1,0:T(8,128)S(1)}, f32[2,32,512]{2,1,0:T(8,128)S(1)}, u32[]{:S(2)}, u32[]{:S(2)}) collective-permute-start(f32[2,32,512]{2,1,0:T(8,128)S(1)} %pad_maximum_fusion.3), channel_id=1, source_target_pairs={{0,96},{1,97},{2,98},{3,99},{4,100},{5,101},{6,102},{7,103},{8,104... | collective-permute-start | bytes 393224 | tf_op jit(solution)/shard_map/ppermute | solution.py:469
  118.9 3.2 %collective-permute-start.22 = (f32[4,32,512]{2,1,0:T(8,128)S(1)}, f32[4,32,512]{2,1,0:T(8,128)S(1)}, u32[]{:S(2)}, u32[]{:S(2)}) collective-permute-start(f32[4,32,512]{2,1,0:T(8,128)S(1)} %pad_maximum_fusion.2), channel_id=1, source_target_pairs={{0,16},{1,17},{2,18},{3,19},{4,20},{5,21},{6,22},{7,23},{8,24},{9,... | collective-permute-start | bytes 786440 | tf_op jit(solution)/shard_map/ppermute | solution.py:469
  127.3 3.6 %collective-permute-done.27 = f32[1,32,256]{2,1,0:T(8,128)S(1)} collective-permute-done((f32[1,32,256]{2,1,0:T(8,128)S(1)}, f32[1,32,256]{2,1,0:T(8,128)S(1)}, u32[]{:S(2)}, u32[]{:S(2)}) %collective-permute-start.27) | collective-permute-done | bytes 32800 | tf_op jit(solution)/shard_map/ppermute | solution.py:469
  130.9 6.4 %basis.1 = (f32[32,4096]{1,0:T(8,128)}, bf16[4096,192]{1,0:T(8,128)(2,1)S(1)}, f32[32,32]{1,0:T(8,128)S(1)}) custom-call(s32[8]{0:T(128)S(1)} %copy-done.17, f32[8,32,512]{2,1,0:T(8,128)S(1)} %pad_maximum_fusion.refs_1_), custom_call_target="tpu_custom_call" | custom-call | tf_op jit(solution)/shard_map/basis/pallas_call | solution.py:107
  137.3 4.4 %collective-permute-start.29 = (f32[4,32,256]{2,1,0:T(8,128)S(1)}, f32[4,32,256]{2,1,0:T(8,128)S(1)}, u32[]{:S(2)}, u32[]{:S(2)}) collective-permute-start(f32[4,32,256]{2,1,0:T(8,128)S(1)} %pair.2), channel_id=1, source_target_pairs={{0,16},{1,17},{2,18},{3,19},{4,20},{5,21},{6,22},{7,23},{8,24},{9,... | collective-permute-start | bytes 393224 | tf_op jit(solution)/shard_map/ppermute | solution.py:469
  142.7 23.6 %collective-permute-done.14.refs_0_ = bf16[2048,1024]{1,0:T(8,128)(2,1)} collective-permute-done((bf16[2048,1024]{1,0:T(8,128)(2,1)}, bf16[2048,1024]{1,0:T(8,128)(2,1)}, u32[]{:S(2)}, u32[]{:S(2)}) %collective-permute-start.14) | collective-permute-done | bytes 4194336 | tf_op jit(solution)/shard_map/ppermute | solution.py:469
  169.5 3.4 %copy-done.5 = f32[1,4096,512]{2,1,0:T(8,128)S(1)} copy-done((f32[1,4096,512]{2,1,0:T(8,128)S(1)}, f32[1,4096,512]{2,1,0:T(8,128)}, u32[]{:S(2)}) %copy-start.5) | copy-done | bytes 8388632
  172.9 4.1 %errors_right.1.rest_0_.refs_2_ = f32[32,512]{1,0:T(8,128)S(1)} custom-call(s32[8]{0:T(128)S(1)} %copy-done.17, f32[8,32,512]{2,1,0:T(8,128)S(1)} %pad_maximum_fusion.refs_1_, f32[4096,512]{1,0:T(8,128)S(1)} %bitcast.77), custom_call_target="tpu_custom_call" | custom-call | tf_op jit(solution)/shard_map/errors_right/pallas_call | solution.py:107
  199.8 7.7 %add_rows.3.refs_0_ = f32[2048,512]{1,0:T(8,128)S(1)} custom-call(f32[4096,512]{1,0:T(8,128)} %bitcast.75, bf16[2048,1024]{1,0:T(8,128)(2,1)} %line.2.refs_1_, bf16[2048,1024]{1,0:T(8,128)(2,1)} %tie.3.refs_2_.refs_9_, bf16[4096,512]{1,0:T(8,128)(2,1)S(1)} %copy-done.2, bf16[4096,512]{1,0:T(8,128)(2,1)S(1)} %copy-done.2), custom_call_target="tpu_custom_call" | custom-call | tf_op jit(solution)/shard_map/add_rows/pallas_call | solution.py:107
  207.6 15.7 %add_rows.4.refs_7_ = f32[4096,512]{1,0:T(8,128)} custom-call(f32[4096,512]{1,0:T(8,128)} %bitcast.76, bf16[2048,1024]{1,0:T(8,128)(2,1)} %line.3.refs_1_, bf16[2048,1024]{1,0:T(8,128)(2,1)} %tie.2.refs_3_.refs_2_, bf16[2048,1024]{1,0:T(8,128)(2,1)} %collective-permute-done.25.refs_4_.refs_3_, bf16[2048,1024]{1,0:T(8,128)(2,1)} %collective-permute-done.34.refs_8_.refs_4_, ...), custom_call_target="tpu_custom_call" | custom-call | tf_op jit(solution)/shard_map/add_rows/pallas_call | solution.py:107
  224.3 9.4 %add_rows.5 = f32[4096,512]{1,0:T(8,128)} custom-call(f32[2048,512]{1,0:T(8,128)S(1)} %add_rows.3.refs_0_, bf16[2048,1024]{1,0:T(8,128)(2,1)} %collective-permute-done.30.refs_1_, bf16[2048,1024]{1,0:T(8,128)(2,1)} %collective-permute-done.31.refs_2_, bf16[4096,512]{1,0:T(8,128)(2,1)} %copy-done, ...), custom_call_target="tpu_custom_call", output_to_operand_aliasing={{}: (7, {})} | custom-call | tf_op jit(solution)/shard_map/add_rows/pallas_call | solution.py:107
  (139 shorter events, 84.0 us)
Async XLA Ops:
  5.9 20.1 %collective-permute-start.9 = (bf16[2048,256]{1,0:T(8,128)(2,1)}, bf16[2048,256]{1,0:T(8,128)(2,1)S(1)}, u32[]{:S(2)}, u32[]{:S(2)}) collective-permute-start(bf16[2048,256]{1,0:T(8,128)(2,1)} %get-tuple-element.9.refs_0_), channel_id=1, source_target_pairs={{0,1},{1,2},{2,3},{3,0},{4,5},{5,6},{6,7},{7,4},{8,9},{9,10},{10,1... | collective-permute-start | bytes 3145736 | tf_op jit(solution)/shard_map/ppermute | solution.py:469
  13.9 9.7 %collective-permute-start.3 = (f32[8,32,256]{2,1,0:T(8,128)S(1)}, f32[8,32,256]{2,1,0:T(8,128)S(1)}, u32[]{:S(2)}, u32[]{:S(2)}) collective-permute-start(f32[8,32,256]{2,1,0:T(8,128)S(1)} %slice.57), channel_id=1, source_target_pairs={{0,12},{1,13},{2,14},{3,15},{4,8},{5,9},{6,10},{7,11},{8,4},{9,5},... | collective-permute-start | bytes 786440 | tf_op jit(solution)/shard_map/ppermute | solution.py:469
  26.0 17.8 %collective-permute-start.10 = (bf16[2048,256]{1,0:T(8,128)(2,1)S(1)}, bf16[2048,256]{1,0:T(8,128)(2,1)S(1)}, u32[]{:S(2)}, u32[]{:S(2)}) collective-permute-start(bf16[2048,256]{1,0:T(8,128)(2,1)S(1)} %collective-permute-done.9.refs_1_), channel_id=1, source_target_pairs={{0,1},{1,2},{2,3},{3,0},{4,5},{5,6},{6,7},{7,4},{8,9},{9,10},{10,1... | collective-permute-start | bytes 3145736 | tf_op jit(solution)/shard_map/ppermute | solution.py:469
  32.1 5.4 %collective-permute-start.6 = (f32[2,32,256]{2,1,0:T(8,128)S(1)}, f32[2,32,256]{2,1,0:T(8,128)S(1)}, u32[]{:S(2)}, u32[]{:S(2)}) collective-permute-start(f32[2,32,256]{2,1,0:T(8,128)S(1)} %slice.61), channel_id=1, source_target_pairs={{0,12},{1,13},{2,14},{3,15},{4,8},{5,9},{6,10},{7,11},{8,4},{9,5},... | collective-permute-start | bytes 196616 | tf_op jit(solution)/shard_map/ppermute | solution.py:469
  33.4 25.4 %collective-permute-start.1 = (bf16[2048,256]{1,0:T(8,128)(2,1)}, bf16[2048,256]{1,0:T(8,128)(2,1)}, u32[]{:S(2)}, u32[]{:S(2)}) collective-permute-start(bf16[2048,256]{1,0:T(8,128)(2,1)} %get-tuple-element.8.refs_0_), channel_id=1, source_target_pairs={{0,3},{1,0},{2,1},{3,2},{4,7},{5,4},{6,5},{7,6},{8,11},{9,8},{10,9... | collective-permute-start | bytes 3145736 | tf_op jit(solution)/shard_map/ppermute | solution.py:469
  35.3 28.3 %collective-permute-start.23 = (bf16[2048,256]{1,0:T(8,128)(2,1)}, bf16[2048,256]{1,0:T(8,128)(2,1)}, u32[]{:S(2)}, u32[]{:S(2)}) collective-permute-start(bf16[2048,256]{1,0:T(8,128)(2,1)} %get-tuple-element.9.refs_0_), channel_id=1, source_target_pairs={{0,3},{1,0},{2,1},{3,2},{4,7},{5,4},{6,5},{7,6},{8,11},{9,8},{10,9... | collective-permute-start | bytes 3145736 | tf_op jit(solution)/shard_map/ppermute | solution.py:469
  41.1 13.3 %collective-permute-start.8 = (f32[32,256]{1,0:T(8,128)S(1)}, f32[32,256]{1,0:T(8,128)S(1)}, u32[]{:S(2)}, u32[]{:S(2)}) collective-permute-start(f32[32,256]{1,0:T(8,128)S(1)} %fusion.1.refs_4_), channel_id=1, source_target_pairs={{0,16},{1,17},{2,18},{3,19},{4,20},{5,21},{6,22},{7,23},{8,24},{9,... | collective-permute-start | bytes 98312 | tf_op jit(solution)/shard_map/ppermute | solution.py:469
  57.9 16.5 %collective-permute-start = (bf16[2048,256]{1,0:T(8,128)(2,1)}, bf16[2048,256]{1,0:T(8,128)(2,1)S(1)}, u32[]{:S(2)}, u32[]{:S(2)}) collective-permute-start(bf16[2048,256]{1,0:T(8,128)(2,1)} %get-tuple-element.8.refs_0_), channel_id=1, source_target_pairs={{0,1},{1,2},{2,3},{3,0},{4,5},{5,6},{6,7},{7,4},{8,9},{9,10},{10,1... | collective-permute-start | bytes 3145736 | tf_op jit(solution)/shard_map/ppermute | solution.py:469
  58.9 15.5 %collective-permute-start.2 = (bf16[2048,256]{1,0:T(8,128)(2,1)}, bf16[2048,256]{1,0:T(8,128)(2,1)S(1)}, u32[]{:S(2)}, u32[]{:S(2)}) collective-permute-start(bf16[2048,256]{1,0:T(8,128)(2,1)} %collective-permute-done.1.refs_2_), channel_id=1, source_target_pairs={{0,3},{1,0},{2,1},{3,2},{4,7},{5,4},{6,5},{7,6},{8,11},{9,8},{10,9... | collective-permute-start | bytes 3145736 | tf_op jit(solution)/shard_map/ppermute | solution.py:469
  61.1 9.7 %collective-permute-start.12 = (f32[2,32,512]{2,1,0:T(8,128)S(1)}, f32[2,32,512]{2,1,0:T(8,128)S(1)}, u32[]{:S(2)}, u32[]{:S(2)}) collective-permute-start(f32[2,32,512]{2,1,0:T(8,128)S(1)} %slice.67), channel_id=1, source_target_pairs={{0,96},{1,97},{2,98},{3,99},{4,100},{5,101},{6,102},{7,103},{8,104... | collective-permute-start | bytes 393224 | tf_op jit(solution)/shard_map/ppermute | solution.py:469
  68.0 55.2 %collective-permute-start.24 = (bf16[2048,1024]{1,0:T(8,128)(2,1)}, bf16[2048,1024]{1,0:T(8,128)(2,1)}, u32[]{:S(2)}, u32[]{:S(2)}) collective-permute-start(bf16[2048,1024]{1,0:T(8,128)(2,1)} %line.3.refs_1_), channel_id=1, source_target_pairs={{0,4},{1,5},{2,6},{3,7},{4,8},{5,9},{6,10},{7,11},{8,12},{9,13},{1... | collective-permute-start | bytes 12582920 | tf_op jit(solution)/shard_map/ppermute | solution.py:469
  69.0 54.3 %collective-permute-start.25 = (bf16[2048,1024]{1,0:T(8,128)(2,1)}, bf16[2048,1024]{1,0:T(8,128)(2,1)}, u32[]{:S(2)}, u32[]{:S(2)}) collective-permute-start(bf16[2048,1024]{1,0:T(8,128)(2,1)} %line.3.refs_1_), channel_id=1, source_target_pairs={{0,12},{1,13},{2,14},{3,15},{4,0},{5,1},{6,2},{7,3},{8,4},{9,5},{1... | collective-permute-start | bytes 12582920 | tf_op jit(solution)/shard_map/ppermute | solution.py:469
  78.8 87.5 %collective-permute-start.14 = (bf16[2048,1024]{1,0:T(8,128)(2,1)}, bf16[2048,1024]{1,0:T(8,128)(2,1)}, u32[]{:S(2)}, u32[]{:S(2)}) collective-permute-start(bf16[2048,1024]{1,0:T(8,128)(2,1)} %line.2.refs_1_), channel_id=1, source_target_pairs={{0,12},{1,13},{2,14},{3,15},{4,0},{5,1},{6,2},{7,3},{8,4},{9,5},{1... | collective-permute-start | bytes 12582920 | tf_op jit(solution)/shard_map/ppermute | solution.py:469
  84.4 5.6 %collective-permute-start.16 = (f32[32,512]{1,0:T(8,128)S(1)}, f32[32,512]{1,0:T(8,128)S(1)}, u32[]{:S(2)}, u32[]{:S(2)}) collective-permute-start(f32[32,512]{1,0:T(8,128)S(1)} %add.488), channel_id=1, source_target_pairs={{0,3},{1,2},{2,1},{3,0},{4,7},{5,6},{6,5},{7,4},{8,11},{9,10},{10,... | collective-permute-start | bytes 196616 | tf_op jit(solution)/shard_map/ppermute | solution.py:469
  90.0 7.8 %collective-permute-start.17 = (f32[32,512]{1,0:T(8,128)S(1)}, f32[32,512]{1,0:T(8,128)S(1)}, u32[]{:S(2)}, u32[]{:S(2)}) collective-permute-start(f32[32,512]{1,0:T(8,128)S(1)} %add.489), channel_id=1, source_target_pairs={{0,16},{1,17},{2,18},{3,19},{4,20},{5,21},{6,22},{7,23},{8,24},{9,... | collective-permute-start | bytes 196616 | tf_op jit(solution)/shard_map/ppermute | solution.py:469
  102.1 5.6 %collective-permute-start.19 = (f32[32,512]{1,0:T(8,128)S(1)}, f32[32,512]{1,0:T(8,128)S(1)}, u32[]{:S(2)}, u32[]{:S(2)}) collective-permute-start(f32[32,512]{1,0:T(8,128)S(1)} %add.490), channel_id=1, source_target_pairs={{0,3},{1,2},{2,1},{3,0},{4,7},{5,6},{6,5},{7,4},{8,11},{9,10},{10,... | collective-permute-start | bytes 196616 | tf_op jit(solution)/shard_map/ppermute | solution.py:469
  112.3 6.6 %collective-permute-start.21 = (f32[2,32,512]{2,1,0:T(8,128)S(1)}, f32[2,32,512]{2,1,0:T(8,128)S(1)}, u32[]{:S(2)}, u32[]{:S(2)}) collective-permute-start(f32[2,32,512]{2,1,0:T(8,128)S(1)} %pad_maximum_fusion.3), channel_id=1, source_target_pairs={{0,96},{1,97},{2,98},{3,99},{4,100},{5,101},{6,102},{7,103},{8,104... | collective-permute-start | bytes 393224 | tf_op jit(solution)/shard_map/ppermute | solution.py:469
  126.4 60.5 %collective-permute-start.34 = (bf16[2048,1024]{1,0:T(8,128)(2,1)}, bf16[2048,1024]{1,0:T(8,128)(2,1)}, u32[]{:S(2)}, u32[]{:S(2)}) collective-permute-start(bf16[2048,1024]{1,0:T(8,128)(2,1)} %tie.2.refs_3_.refs_2_), channel_id=1, source_target_pairs={{0,4},{1,5},{2,6},{3,7},{4,8},{5,9},{6,10},{7,11},{8,12},{9,13},{1... | collective-permute-start | bytes 12582920 | tf_op jit(solution)/shard_map/ppermute | solution.py:469
  130.9 6.5 %collective-permute-start.28 = (f32[2,32,256]{2,1,0:T(8,128)S(1)}, f32[2,32,256]{2,1,0:T(8,128)S(1)}, u32[]{:S(2)}, u32[]{:S(2)}) collective-permute-start(f32[2,32,256]{2,1,0:T(8,128)S(1)} %constant_dynamic-update-slice_fusion.a), channel_id=1, source_target_pairs={{0,3},{1,2},{2,1},{3,0},{4,7},{5,6},{6,5},{7,4},{8,11},{9,10},{10,... | collective-permute-start | bytes 196616 | tf_op jit(solution)/shard_map/ppermute | solution.py:469
  141.7 82.6 %collective-permute-start.30 = (bf16[2048,1024]{1,0:T(8,128)(2,1)}, bf16[2048,1024]{1,0:T(8,128)(2,1)}, u32[]{:S(2)}, u32[]{:S(2)}) collective-permute-start(bf16[2048,1024]{1,0:T(8,128)(2,1)} %line.2.refs_1_), channel_id=1, source_target_pairs={{0,4},{1,5},{2,6},{3,7},{4,8},{5,9},{6,10},{7,11},{8,12},{9,13},{1... | collective-permute-start | bytes 12582920 | tf_op jit(solution)/shard_map/ppermute | solution.py:469
  166.3 58.0 %collective-permute-start.31 = (bf16[2048,1024]{1,0:T(8,128)(2,1)}, bf16[2048,1024]{1,0:T(8,128)(2,1)}, u32[]{:S(2)}, u32[]{:S(2)}) collective-permute-start(bf16[2048,1024]{1,0:T(8,128)(2,1)} %tie.3.refs_2_.refs_9_), channel_id=1, source_target_pairs={{0,12},{1,13},{2,14},{3,15},{4,0},{5,1},{6,2},{7,3},{8,4},{9,5},{1... | collective-permute-start | bytes 12582920 | tf_op jit(solution)/shard_map/ppermute | solution.py:469
  169.2 7.8 %collective-permute-start.32 = (f32[4,32,256]{2,1,0:T(8,128)}, f32[4,32,256]{2,1,0:T(8,128)S(1)}, u32[]{:S(2)}, u32[]{:S(2)}) collective-permute-start(f32[4,32,256]{2,1,0:T(8,128)} %copy-done.14), channel_id=1, source_target_pairs={{0,1},{1,0},{2,3},{3,2},{4,5},{5,4},{6,7},{7,6},{8,9},{9,8},{10,11... | collective-permute-start | bytes 393224 | tf_op jit(solution)/shard_map/ppermute | solution.py:469
  177.1 9.8 %collective-permute-start.33 = (f32[8,32,256]{2,1,0:T(8,128)S(1)}, f32[8,32,256]{2,1,0:T(8,128)S(1)}, u32[]{:S(2)}, u32[]{:S(2)}) collective-permute-start(f32[8,32,256]{2,1,0:T(8,128)S(1)} %pair.3), channel_id=1, source_target_pairs={{0,3},{1,2},{2,1},{3,0},{4,7},{5,6},{6,5},{7,4},{8,11},{9,10},{10,... | collective-permute-start | bytes 786440 | tf_op jit(solution)/shard_map/ppermute | solution.py:469
  197.3 10.2 %collective-permute-start.37 = (f32[32,512]{1,0:T(8,128)S(1)}, f32[32,512]{1,0:T(8,128)S(1)}, u32[]{:S(2)}, u32[]{:S(2)}) collective-permute-start(f32[32,512]{1,0:T(8,128)S(1)} %add.556), channel_id=1, source_target_pairs={{0,96},{1,97},{2,98},{3,99},{4,100},{5,101},{6,102},{7,103},{8,104... | collective-permute-start | bytes 196616 | tf_op jit(solution)/shard_map/ppermute | solution.py:469
  (33 other events, 187.6 us)

commit v3 on v2

--- a/solution.py
+++ b/solution.py
@@ -111,27 +111,18 @@
     return jax.ShapeDtypeStruct(dims, dtype)
 
 
-def turn_kernel(acts, unit0, unit1):
-    half = PART // 512
-    for dst, inside in ((unit0, pl.program_id(0) < half), (unit1, pl.program_id(0) >= half)):
-
-        @pl.when(inside)
-        def _(dst=dst):
-            dst[...] = acts[...].T
+def turn_kernel(acts, out):
+    out[...] = acts[...].T
 
 
 def turn(acts):
-    half = PART // 512
     return kernel_call(
         turn_kernel,
         "turn",
-        (2 * half,),
+        (8,),
         [pl.BlockSpec((UNIT, 512), lambda i: (0, i))],
-        [
-            pl.BlockSpec((512, UNIT), lambda i: (jnp.minimum(i, half - 1), 0)),
-            pl.BlockSpec((512, UNIT), lambda i: (jnp.maximum(i - half, 0), 0)),
-        ],
-        [shape(PART, UNIT, dtype=BF16)] * 2,
+        pl.BlockSpec((512, UNIT), lambda i: (i, 0)),
+        shape(2 * PART, UNIT, dtype=BF16),
     )(acts)
 
 
@@ -140,16 +131,17 @@
         refs[-1][:, k * UNIT : (k + 1) * UNIT] = ref[...]
 
 
-def join_line(units, *after):
+def join_line(chunk, units, far, *after):
+    skip = chunk * (PART // 512)
     return kernel_call(
         line_kernel,
         "line",
         (PART // 512,),
-        [pl.BlockSpec((512, UNIT), lambda i: (i, 0))] * 4,
+        [pl.BlockSpec((512, UNIT), lambda i: (skip + i, 0))] * 3 + [pl.BlockSpec((512, UNIT), lambda i: (i, 0))],
         pl.BlockSpec((512, 4 * UNIT), lambda i: (i, 0)),
         shape(PART, 4 * UNIT, dtype=BF16),
         after=after,
-    )(*units)
+    )(*units, far)
 
 
 def arrange_kernel(order, g0, g1, g2, g3, out):
@@ -229,7 +221,7 @@
     out[0] = part[0] + fold(dot(three, acts[...], NN))
 
 
-def left_terms(order, u, part, acts):
+def left_terms(order, u, part, acts, *after):
     return kernel_call(
         left_kernel,
         "left_terms",
@@ -242,6 +234,7 @@
         pl.BlockSpec((1, RANK, 512), lambda m, o: (m, 0, 0)),
         shape(8, RANK, 512),
         prefetch=1,
+        after=after,
     )(order, u, part, acts)
 
 
@@ -450,6 +443,22 @@
     )(a, *after)
 
 
+def halve_kernel(u, r, *rest):
+    rest[-1][...] = u[: r.shape[0]] + r[...]
+
+
+def halve(u, r, *after):
+    vmem = pl.BlockSpec(memory_space=pltpu.VMEM)
+    return pl.pallas_call(
+        halve_kernel,
+        in_specs=[vmem] * 2 + [pl.BlockSpec(memory_space=pl.ANY)] * len(after),
+        out_specs=vmem,
+        out_shape=jax.ShapeDtypeStruct(r.shape, r.dtype),
+        compiler_params=pltpu.CompilerParams(vmem_limit_bytes=16 * 2**20),
+        name="halve",
+    )(u, r, *after)
+
+
 def pair_kernel(a, b, *rest):
     n = a.shape[0]
     rest[-1][:n] = a[...]
@@ -457,8 +466,11 @@
 
 
 def pair(a, b, *others):
+    vmem = pl.BlockSpec(memory_space=pltpu.VMEM)
     return pl.pallas_call(
         pair_kernel,
+        in_specs=[vmem] * 2 + [pl.BlockSpec(memory_space=pl.ANY)] * len(others),
+        out_specs=vmem,
         out_shape=jax.ShapeDtypeStruct((2 * a.shape[0],) + a.shape[1:], a.dtype),
         compiler_params=pltpu.CompilerParams(vmem_limit_bytes=16 * 2**20),
         name="pair",
@@ -503,30 +515,30 @@
     in_kept = int_array([4 * place(b, q) + place(a, p) for a in codes(p) for b in codes(q)])
     factor = previous_factor.T
     units = turn(activations)
-    above0, below0 = send(units[0], PUP), send(units[0], PDOWN)
-    far0, below1 = send(above0, PUP), send(units[1], PDOWN)
-    above1, far1 = send(units[1], PUP), send(below1, PDOWN)
+    above, below = send(units, PUP), send(units, PDOWN)
+    far0, far1 = send(above[:PART], PUP), send(below[PART:], PDOWN)
+    units = (units, above, below)
 
     u = tokens(by_code_q, factor, output_grads)
-    u = u[:8] + send(u[8:], QOUT)
+    part = errors_left(by_rep, factor, errors)
+    u = halve(u, send(u[8:], QOUT), part)
     u = u[:4] + send(u[4:], QIN)
     u = send(u, CORE)
     u = u[:2] + send(u[2:], QOUT)
     u = u[0] + send(u[1], QIN)
-    line0 = join_line((units[0], above0, below0, far0), u)
+    line0 = join_line(0, units, far0, u, far1)
     top0, bottom0 = send(line0, QUP), send(line0, QDOWN)
     u = send(u, CORE)
-    part = errors_left(by_rep, factor, errors, far0)
-    left = left_terms(by_rep, u, part, activations)
+    left = left_terms(by_rep, u, part, activations, line0)
     left = left[:4] + send(left[4:], CORE)
     left = left[:2] + send(left[2:], XOUT)
-    left = left[0] + send(left[1], XIN)
-    line1 = join_line((units[1], above1, below1, far1), left)
+    line1 = join_line(1, units, far1, left)
     top1, bottom1 = send(line1, QUP), send(line1, QDOWN)
+    left = halve(left, send(left[1:], XIN), line1)[0]
     left = left + send(left, PIN)
     left = left + send(left, POUT)
     left = send(left, CORE)
-    top0 = tie(top0, left)
+    top0 = tie(top0, left, bottom0)
     opposite0 = send(top0, QUP)
     left = left + send(left, PIN)
     left = left + send(left, POUT)
@@ -543,17 +555,17 @@
     w = cat(w, send(w, PIN))
     w = pair(w, send(w, POUT), inverse)
     w = send(w, CORE)
-    bottom1 = tie(bottom1, w)
+    sum0 = add_rows(errors, 0, ((line0, 0), (top0, 1), (bottom0, 2)), kept, 0, PART)
+    bottom1 = tie(bottom1, w, sum0)
     opposite1 = send(bottom1, QDOWN)
-    w = pair(w, send(w, PIN), part)
+    sum1 = add_rows(errors, PART // STRIP, ((line1, 0), (bottom1, 2)), kept, 0, PART)
+    w = pair(w, send(w, PIN), part, sum0, sum1, opposite0)
     w = cat(w, send(w, POUT))
-    right = right_terms(in_kept, w, part, inverse, kept, opposite0, bottom1)
+    right = right_terms(in_kept, w, part, inverse, kept)
     for perm in (CORE, XIN, XOUT):
         right = right + send(right, perm)
     update = (six, right)
-    sum1 = add_rows(errors, PART // STRIP, ((line1, 0), (bottom1, 2)), kept, 0, PART)
-    blocks = ((line0, 0), (top0, 1), (bottom0, 2), (opposite0, 3))
-    out = add_rows(errors, 0, blocks, kept, 0, 2 * PART, update)
+    out = add_rows(sum0, 0, ((opposite0, 3),), kept, 0, 2 * PART, update)
     out = add_rows(sum1, 0, ((top1, 1), (opposite1, 3)), kept, PART, 2 * PART, update, out)
     return (out[None], basis.T, right.T)
 

time: 235 us -> 230 us (0.979)
  local copies, waits for them, and re-layouts: 18.6 us -> 29.6 us
  waiting for transfers between devices: 79.2 us -> 69.9 us
  Pallas kernels: 75.5 us -> 71.8 us
  starting transfers between devices: 59.1 us -> 56.1 us
    ppermute x38 -> x36, waiting for transfers between devices: 79.2 us -> 69.9 us  [send(): return lax.ppermute(a, ALL, perm)]
    unnamed x39 -> x59, local copies, waits for them, and re-layouts: 17.6 us -> 26 us
    pallas_call x14 -> x15, Pallas kernels: 75.5 us -> 71.8 us  [kernel_call(): return lambda *args: call(*args, *after)]
    ppermute x38 -> x36, starting transfers between devices: 59.1 us -> 56.1 us  [send(): return lax.ppermute(a, ALL, perm)]
    slice x1 -> x4, local copies, waits for them, and re-layouts: 0.04 us -> 2.64 us  [the longest x2 2.59 us: local(): far0, far1 = (send(above[:PART], PUP), send(below[PART:], PDOWN))]
  transfers between devices with their start and end apart: 38 -> 36, of which waited for: 23 -> 21; matrix products, arithmetic and copies ran while one was open for 1% -> 2% of each run, Pallas kernels for 27% -> 26%
where the time goes in v3:
time: 230 us; the launch traced here: 229 us
  Pallas kernels  71.8 us (31%)
  waiting for transfers between devices  69.9 us (30%)
  starting transfers between devices  56.1 us (24%)
  local copies, waits for them, and re-layouts  29.6 us (13%)
    pallas_call x15, Pallas kernels, kernel_call(): return lambda *args: call(*args, *after)  71.8 us
    ppermute x36, waiting for transfers between devices, send(): return lax.ppermute(a, ALL, perm)  69.9 us
    ppermute x36, starting transfers between devices, send(): return lax.ppermute(a, ALL, perm)  56.1 us
    unnamed x59, local copies, waits for them, and re-layouts  26 us
  transfers between devices with their start and end apart: 36, of which 21 were waited for; matrix products, arithmetic and copies ran while one was open for 2% of the time, Pallas kernels for 26%

profile of v3, /device:TPU:1, one launch (start us, length us, event | category | flops | bytes accessed | tf_op | source)
XLA Modules:
  0.0 229.0 jit_solution(8923945799987019841)
XLA Ops:
  3.4 4.7 %collective-permute-start.1 = (bf16[4096,256]{1,0:T(8,128)(2,1)S(1)}, bf16[4096,256]{1,0:T(8,128)(2,1)}, u32[]{:S(2)}, u32[]{:S(2)}) collective-permute-start(bf16[4096,256]{1,0:T(8,128)(2,1)S(1)} %turn.1.refs_0_), channel_id=1, source_target_pairs={{0,3},{1,0},{2,1},{3,2},{4,7},{5,4},{6,5},{7,6},{8,11},{9,8},{10,9... | collective-permute-start | bytes 6291464 | tf_op jit(solution)/shard_map/ppermute | solution.py:481
  16.3 9.5 %errors_left.1.rest_0_.refs_2_ = f32[8,32,512]{2,1,0:T(8,128)} custom-call(s32[8]{0:T(128)} %stack.184.refs_0_, f32[32,512]{1,0:T(8,128)} %bitcast.75, f32[4096,512]{1,0:T(8,128)} %bitcast.70), custom_call_target="tpu_custom_call" | custom-call | tf_op jit(solution)/shard_map/errors_left/pallas_call | solution.py:107
  27.2 6.7 %collective-permute-done.1.refs_2_ = bf16[4096,256]{1,0:T(8,128)(2,1)} collective-permute-done((bf16[4096,256]{1,0:T(8,128)(2,1)S(1)}, bf16[4096,256]{1,0:T(8,128)(2,1)}, u32[]{:S(2)}, u32[]{:S(2)}) %collective-permute-start.1) | collective-permute-done | bytes 2097184 | tf_op jit(solution)/shard_map/ppermute | solution.py:481
  35.2 3.6 %collective-permute-start.2 = (bf16[2048,256]{1,0:T(8,128)(2,1)S(1)}, bf16[2048,256]{1,0:T(8,128)(2,1)S(1)}, u32[]{:S(2)}, u32[]{:S(2)}) collective-permute-start(bf16[2048,256]{1,0:T(8,128)(2,1)S(1)} %slice.56), channel_id=1, source_target_pairs={{0,3},{1,0},{2,1},{3,2},{4,7},{5,4},{6,5},{7,6},{8,11},{9,8},{10,9... | collective-permute-start | bytes 3145736 | tf_op jit(solution)/shard_map/ppermute | solution.py:481
  42.0 2.9 %collective-permute-start.6 = (f32[2,32,256]{2,1,0:T(8,128)S(1)}, f32[2,32,256]{2,1,0:T(8,128)S(1)}, u32[]{:S(2)}, u32[]{:S(2)}) collective-permute-start(f32[2,32,256]{2,1,0:T(8,128)S(1)} %slice.61), channel_id=1, source_target_pairs={{0,12},{1,13},{2,14},{3,15},{4,8},{5,9},{6,10},{7,11},{8,4},{9,5},... | collective-permute-start | bytes 196616 | tf_op jit(solution)/shard_map/ppermute | solution.py:481
  47.7 3.0 %collective-permute-done.7 = f32[32,256]{1,0:T(8,128)S(1)} collective-permute-done((f32[32,256]{1,0:T(8,128)S(1)}, f32[32,256]{1,0:T(8,128)S(1)}, u32[]{:S(2)}, u32[]{:S(2)}) %collective-permute-start.7) | collective-permute-done | bytes 32800 | tf_op jit(solution)/shard_map/ppermute | solution.py:481
  70.7 4.4 %line.3.rest_0_.refs_1_ = bf16[2048,1024]{1,0:T(8,128)(2,1)} custom-call(bf16[4096,256]{1,0:T(8,128)(2,1)S(1)} %copy-done.20, bf16[4096,256]{1,0:T(8,128)(2,1)} %collective-permute-done.refs_1_, bf16[4096,256]{1,0:T(8,128)(2,1)} %collective-permute-done.1.refs_2_, bf16[2048,256]{1,0:T(8,128)(2,1)S(1)} %collective-permute-done.2.refs_5_.refs_3_, ...), custom_call_target="tpu_custom_call" | custom-call | tf_op jit(solution)/shard_map/line/pallas_call | solution.py:107
  75.3 3.4 %collective-permute-done.13.r = f32[1,32,512]{2,1,0:T(8,128)S(1)} collective-permute-done((f32[1,32,512]{2,1,0:T(8,128)S(1)}, f32[1,32,512]{2,1,0:T(8,128)S(1)}, u32[]{:S(2)}, u32[]{:S(2)}) %collective-permute-start.13) | collective-permute-done | bytes 65568 | tf_op jit(solution)/shard_map/ppermute | solution.py:481
  84.4 3.9 %collective-permute-start.15 = (f32[32,512]{1,0:T(8,128)S(1)}, f32[32,512]{1,0:T(8,128)S(1)}, u32[]{:S(2)}, u32[]{:S(2)}) collective-permute-start(f32[32,512]{1,0:T(8,128)S(1)} %bitcast_add_fusion), channel_id=1, source_target_pairs={{0,3},{1,2},{2,1},{3,0},{4,7},{5,6},{6,5},{7,4},{8,11},{9,10},{10,... | collective-permute-start | bytes 196616 | tf_op jit(solution)/shard_map/ppermute | solution.py:481
  91.1 5.5 %collective-permute-start.16 = (f32[32,512]{1,0:T(8,128)S(1)}, f32[32,512]{1,0:T(8,128)S(1)}, u32[]{:S(2)}, u32[]{:S(2)}) collective-permute-start(f32[32,512]{1,0:T(8,128)S(1)} %add.481), channel_id=1, source_target_pairs={{0,16},{1,17},{2,18},{3,19},{4,20},{5,21},{6,22},{7,23},{8,24},{9,... | collective-permute-start | bytes 196616 | tf_op jit(solution)/shard_map/ppermute | solution.py:481
  97.4 4.3 %collective-permute-done.17 = f32[32,512]{1,0:T(8,128)S(1)} collective-permute-done((f32[32,512]{1,0:T(8,128)S(1)}, f32[32,512]{1,0:T(8,128)S(1)}, u32[]{:S(2)}, u32[]{:S(2)}) %collective-permute-start.17) | collective-permute-done | bytes 65568 | tf_op jit(solution)/shard_map/ppermute | solution.py:481
  101.9 5.3 %collective-permute-done.18 = f32[32,512]{1,0:T(8,128)S(1)} collective-permute-done((f32[32,512]{1,0:T(8,128)S(1)}, f32[32,512]{1,0:T(8,128)S(1)}, u32[]{:S(2)}, u32[]{:S(2)}) %collective-permute-start.18) | collective-permute-done | bytes 65568 | tf_op jit(solution)/shard_map/ppermute | solution.py:481
  107.3 3.5 %collective-permute-done.19 = f32[1,32,512]{2,1,0:T(8,128)S(1)} collective-permute-done((f32[1,32,512]{2,1,0:T(8,128)S(1)}, f32[1,32,512]{2,1,0:T(8,128)S(1)}, u32[]{:S(2)}, u32[]{:S(2)}) %collective-permute-start.19) | collective-permute-done | bytes 65568 | tf_op jit(solution)/shard_map/ppermute | solution.py:481
  115.9 3.9 %collective-permute-start.21 = (f32[4,32,512]{2,1,0:T(8,128)S(1)}, f32[4,32,512]{2,1,0:T(8,128)S(1)}, u32[]{:S(2)}, u32[]{:S(2)}) collective-permute-start(f32[4,32,512]{2,1,0:T(8,128)S(1)} %pad_maximum_fusion.2), channel_id=1, source_target_pairs={{0,16},{1,17},{2,18},{3,19},{4,20},{5,21},{6,22},{7,23},{8,24},{9,... | collective-permute-start | bytes 786440 | tf_op jit(solution)/shard_map/ppermute | solution.py:481
  128.1 3.6 %collective-permute-done.25 = f32[1,32,256]{2,1,0:T(8,128)S(1)} collective-permute-done((f32[1,32,256]{2,1,0:T(8,128)S(1)}, f32[1,32,256]{2,1,0:T(8,128)S(1)}, u32[]{:S(2)}, u32[]{:S(2)}) %collective-permute-start.25) | collective-permute-done | bytes 32800 | tf_op jit(solution)/shard_map/ppermute | solution.py:481
  134.3 6.4 %basis.1 = (f32[32,4096]{1,0:T(8,128)}, bf16[4096,192]{1,0:T(8,128)(2,1)S(1)}, f32[32,32]{1,0:T(8,128)S(1)}) custom-call(s32[8]{0:T(128)S(1)} %copy-done.27, f32[8,32,512]{2,1,0:T(8,128)S(1)} %pad_maximum_fusion.refs_1_), custom_call_target="tpu_custom_call" | custom-call | tf_op jit(solution)/shard_map/basis/pallas_call | solution.py:107
  149.3 9.7 %add_rows.4.refs_2_.rest_1_.refs_0_ = f32[2048,512]{1,0:T(8,128)S(1)} custom-call(f32[4096,512]{1,0:T(8,128)} %bitcast.71, bf16[2048,1024]{1,0:T(8,128)(2,1)S(1)} %copy-done.13, bf16[2048,1024]{1,0:T(8,128)(2,1)S(1)} %copy-done.16, bf16[2048,1024]{1,0:T(8,128)(2,1)} %collective-permute-done.23.refs_2_.refs_4_.refs_3_, bf16[4096,512]{1,0:T(8,128)(2,1)} %copy-done, ...), custom_call_target="tpu_custom_call" | custom-call | tf_op jit(solution)/shard_map/add_rows/pallas_call | solution.py:107
  162.6 3.8 %copy-done.6 = f32[1,4096,512]{2,1,0:T(8,128)S(1)} copy-done((f32[1,4096,512]{2,1,0:T(8,128)S(1)}, f32[1,4096,512]{2,1,0:T(8,128)}, u32[]{:S(2)}) %copy-start.6) | copy-done | bytes 8388632
  166.3 4.1 %errors_right.1.rest_0_.refs_2_ = f32[32,512]{1,0:T(8,128)S(1)} custom-call(s32[8]{0:T(128)S(1)} %copy-done.27, f32[8,32,512]{2,1,0:T(8,128)S(1)} %pad_maximum_fusion.refs_1_, f32[4096,512]{1,0:T(8,128)S(1)} %bitcast.73), custom_call_target="tpu_custom_call" | custom-call | tf_op jit(solution)/shard_map/errors_right/pallas_call | solution.py:107
  170.5 7.8 %add_rows.5.rest_2_.refs_0_ = f32[2048,512]{1,0:T(8,128)S(1)} custom-call(f32[4096,512]{1,0:T(8,128)} %bitcast.72, bf16[2048,1024]{1,0:T(8,128)(2,1)} %line.3.rest_0_.refs_1_, bf16[2048,1024]{1,0:T(8,128)(2,1)} %tie.3.refs_2_, bf16[4096,512]{1,0:T(8,128)(2,1)S(1)} %copy-done.1, bf16[4096,512]{1,0:T(8,128)(2,1)S(1)} %copy-done.1), custom_call_target="tpu_custom_call" | custom-call | tf_op jit(solution)/shard_map/add_rows/pallas_call | solution.py:107
  182.2 7.7 %collective-permute-done.32 = f32[8,32,256]{2,1,0:T(8,128)S(1)} collective-permute-done((f32[8,32,256]{2,1,0:T(8,128)S(1)}, f32[8,32,256]{2,1,0:T(8,128)S(1)}, u32[]{:S(2)}, u32[]{:S(2)}) %collective-permute-start.32) | collective-permute-done | bytes 262176 | tf_op jit(solution)/shard_map/ppermute | solution.py:481
  205.1 6.6 %add_rows.6.refs_7_ = f32[4096,512]{1,0:T(8,128)} custom-call(f32[2048,512]{1,0:T(8,128)S(1)} %copy-done.9, bf16[2048,1024]{1,0:T(8,128)(2,1)} %collective-permute-done.31.rest_3_.refs_1_, bf16[4096,512]{1,0:T(8,128)(2,1)S(1)} %copy-done.3, bf16[4096,192]{1,0:T(8,128)(2,1)S(1)} %get-tuple-element.7.refs_3_.refs_5_, f32[32,512]{1,0:T(8,128)S(1)} %add.549.refs_4_.refs_6_), custom_call_target="tpu_custom_call" | custom-call | tf_op jit(solution)/shard_map/add_rows/pallas_call | solution.py:107
  211.7 7.9 %collective-permute-done.28.refs_1_ = bf16[2048,1024]{1,0:T(8,128)(2,1)} collective-permute-done((bf16[2048,1024]{1,0:T(8,128)(2,1)}, bf16[2048,1024]{1,0:T(8,128)(2,1)}, u32[]{:S(2)}, u32[]{:S(2)}) %collective-permute-start.28) | collective-permute-done | bytes 4194336 | tf_op jit(solution)/shard_map/ppermute | solution.py:481
  219.5 9.4 %add_rows.7 = f32[4096,512]{1,0:T(8,128)} custom-call(f32[2048,512]{1,0:T(8,128)S(1)} %copy-done.11, bf16[2048,1024]{1,0:T(8,128)(2,1)} %collective-permute-done.28.refs_1_, bf16[2048,1024]{1,0:T(8,128)(2,1)} %collective-permute-done.29.refs_2_, bf16[4096,512]{1,0:T(8,128)(2,1)} %copy-done, ...), custom_call_target="tpu_custom_call", output_to_operand_aliasing={{}: (7, {})} | custom-call | tf_op jit(solution)/shard_map/add_rows/pallas_call | solution.py:107
  (158 shorter events, 96.2 us)
Async XLA Ops:
  3.4 30.4 %collective-permute-start.1 = (bf16[4096,256]{1,0:T(8,128)(2,1)S(1)}, bf16[4096,256]{1,0:T(8,128)(2,1)}, u32[]{:S(2)}, u32[]{:S(2)}) collective-permute-start(bf16[4096,256]{1,0:T(8,128)(2,1)S(1)} %turn.1.refs_0_), channel_id=1, source_target_pairs={{0,3},{1,0},{2,1},{3,2},{4,7},{5,4},{6,5},{7,6},{8,11},{9,8},{10,9... | collective-permute-start | bytes 6291464 | tf_op jit(solution)/shard_map/ppermute | solution.py:481
  8.1 30.7 %collective-permute-start = (bf16[4096,256]{1,0:T(8,128)(2,1)S(1)}, bf16[4096,256]{1,0:T(8,128)(2,1)}, u32[]{:S(2)}, u32[]{:S(2)}) collective-permute-start(bf16[4096,256]{1,0:T(8,128)(2,1)S(1)} %turn.1.refs_0_), channel_id=1, source_target_pairs={{0,1},{1,2},{2,3},{3,0},{4,5},{5,6},{6,7},{7,4},{8,9},{9,10},{10,1... | collective-permute-start | bytes 6291464 | tf_op jit(solution)/shard_map/ppermute | solution.py:481
  12.8 13.0 %collective-permute-start.3 = (f32[8,32,256]{2,1,0:T(8,128)S(1)}, f32[8,32,256]{2,1,0:T(8,128)S(1)}, u32[]{:S(2)}, u32[]{:S(2)}) collective-permute-start(f32[8,32,256]{2,1,0:T(8,128)S(1)} %slice.57), channel_id=1, source_target_pairs={{0,12},{1,13},{2,14},{3,15},{4,8},{5,9},{6,10},{7,11},{8,4},{9,5},... | collective-permute-start | bytes 786440 | tf_op jit(solution)/shard_map/ppermute | solution.py:481
  27.1 13.1 %collective-permute-start.4 = (f32[4,32,256]{2,1,0:T(8,128)S(1)}, f32[4,32,256]{2,1,0:T(8,128)S(1)}, u32[]{:S(2)}, u32[]{:S(2)}) collective-permute-start(f32[4,32,256]{2,1,0:T(8,128)S(1)} %slice.59), channel_id=1, source_target_pairs={{0,4},{1,5},{2,6},{3,7},{4,0},{5,1},{6,2},{7,3},{8,12},{9,13},{10,... | collective-permute-start | bytes 393224 | tf_op jit(solution)/shard_map/ppermute | solution.py:481
  35.2 18.4 %collective-permute-start.2 = (bf16[2048,256]{1,0:T(8,128)(2,1)S(1)}, bf16[2048,256]{1,0:T(8,128)(2,1)S(1)}, u32[]{:S(2)}, u32[]{:S(2)}) collective-permute-start(bf16[2048,256]{1,0:T(8,128)(2,1)S(1)} %slice.56), channel_id=1, source_target_pairs={{0,3},{1,0},{2,1},{3,2},{4,7},{5,4},{6,5},{7,6},{8,11},{9,8},{10,9... | collective-permute-start | bytes 3145736 | tf_op jit(solution)/shard_map/ppermute | solution.py:481
  40.1 15.9 %collective-permute-start.9 = (bf16[2048,256]{1,0:T(8,128)(2,1)S(1)}, bf16[2048,256]{1,0:T(8,128)(2,1)S(1)}, u32[]{:S(2)}, u32[]{:S(2)}) collective-permute-start(bf16[2048,256]{1,0:T(8,128)(2,1)S(1)} %slice.64), channel_id=1, source_target_pairs={{0,1},{1,2},{2,3},{3,0},{4,5},{5,6},{6,7},{7,4},{8,9},{9,10},{10,1... | collective-permute-start | bytes 3145736 | tf_op jit(solution)/shard_map/ppermute | solution.py:481
  42.0 5.6 %collective-permute-start.6 = (f32[2,32,256]{2,1,0:T(8,128)S(1)}, f32[2,32,256]{2,1,0:T(8,128)S(1)}, u32[]{:S(2)}, u32[]{:S(2)}) collective-permute-start(f32[2,32,256]{2,1,0:T(8,128)S(1)} %slice.61), channel_id=1, source_target_pairs={{0,12},{1,13},{2,14},{3,15},{4,8},{5,9},{6,10},{7,11},{8,4},{9,5},... | collective-permute-start | bytes 196616 | tf_op jit(solution)/shard_map/ppermute | solution.py:481
  50.8 7.8 %collective-permute-start.8 = (f32[32,256]{1,0:T(8,128)S(1)}, f32[32,256]{1,0:T(8,128)S(1)}, u32[]{:S(2)}, u32[]{:S(2)}) collective-permute-start(f32[32,256]{1,0:T(8,128)S(1)} %fusion.refs_4_), channel_id=1, source_target_pairs={{0,16},{1,17},{2,18},{3,19},{4,20},{5,21},{6,22},{7,23},{8,24},{9,... | collective-permute-start | bytes 98312 | tf_op jit(solution)/shard_map/ppermute | solution.py:481
  62.5 57.4 %collective-permute-start.22 = (bf16[2048,1024]{1,0:T(8,128)(2,1)S(1)}, bf16[2048,1024]{1,0:T(8,128)(2,1)S(1)}, u32[]{:S(2)}, u32[]{:S(2)}) collective-permute-start(bf16[2048,1024]{1,0:T(8,128)(2,1)S(1)} %line.2.refs_4_.refs_1_), channel_id=1, source_target_pairs={{0,4},{1,5},{2,6},{3,7},{4,8},{5,9},{6,10},{7,11},{8,12},{9,13},{1... | collective-permute-start | bytes 12582920 | tf_op jit(solution)/shard_map/ppermute | solution.py:481
  62.5 59.4 %collective-permute-start.23 = (bf16[2048,1024]{1,0:T(8,128)(2,1)S(1)}, bf16[2048,1024]{1,0:T(8,128)(2,1)}, u32[]{:S(2)}, u32[]{:S(2)}) collective-permute-start(bf16[2048,1024]{1,0:T(8,128)(2,1)S(1)} %line.2.refs_4_.refs_1_), channel_id=1, source_target_pairs={{0,12},{1,13},{2,14},{3,15},{4,0},{5,1},{6,2},{7,3},{8,4},{9,5},{1... | collective-permute-start | bytes 12582920 | tf_op jit(solution)/shard_map/ppermute | solution.py:481
  65.3 5.4 %collective-permute-start.11 = (f32[2,32,512]{2,1,0:T(8,128)S(1)}, f32[2,32,512]{2,1,0:T(8,128)S(1)}, u32[]{:S(2)}, u32[]{:S(2)}) collective-permute-start(f32[2,32,512]{2,1,0:T(8,128)S(1)} %slice.68), channel_id=1, source_target_pairs={{0,96},{1,97},{2,98},{3,99},{4,100},{5,101},{6,102},{7,103},{8,104... | collective-permute-start | bytes 393224 | tf_op jit(solution)/shard_map/ppermute | solution.py:481
  75.1 86.1 %collective-permute-start.12 = (bf16[2048,1024]{1,0:T(8,128)(2,1)}, bf16[2048,1024]{1,0:T(8,128)(2,1)}, u32[]{:S(2)}, u32[]{:S(2)}) collective-permute-start(bf16[2048,1024]{1,0:T(8,128)(2,1)} %line.3.rest_0_.refs_1_), channel_id=1, source_target_pairs={{0,12},{1,13},{2,14},{3,15},{4,0},{5,1},{6,2},{7,3},{8,4},{9,5},{1... | collective-permute-start | bytes 12582920 | tf_op jit(solution)/shard_map/ppermute | solution.py:481
  78.7 5.7 %collective-permute-start.14 = (f32[32,512]{1,0:T(8,128)S(1)}, f32[32,512]{1,0:T(8,128)S(1)}, u32[]{:S(2)}, u32[]{:S(2)}) collective-permute-start(f32[32,512]{1,0:T(8,128)S(1)} %bitcast.77), channel_id=1, source_target_pairs={{0,1},{1,0},{2,3},{3,2},{4,5},{5,4},{6,7},{7,6},{8,9},{9,8},{10,11... | collective-permute-start | bytes 196616 | tf_op jit(solution)/shard_map/ppermute | solution.py:481
  84.4 6.6 %collective-permute-start.15 = (f32[32,512]{1,0:T(8,128)S(1)}, f32[32,512]{1,0:T(8,128)S(1)}, u32[]{:S(2)}, u32[]{:S(2)}) collective-permute-start(f32[32,512]{1,0:T(8,128)S(1)} %bitcast_add_fusion), channel_id=1, source_target_pairs={{0,3},{1,2},{2,1},{3,0},{4,7},{5,6},{6,5},{7,4},{8,11},{9,10},{10,... | collective-permute-start | bytes 196616 | tf_op jit(solution)/shard_map/ppermute | solution.py:481
  91.1 6.4 %collective-permute-start.16 = (f32[32,512]{1,0:T(8,128)S(1)}, f32[32,512]{1,0:T(8,128)S(1)}, u32[]{:S(2)}, u32[]{:S(2)}) collective-permute-start(f32[32,512]{1,0:T(8,128)S(1)} %add.481), channel_id=1, source_target_pairs={{0,16},{1,17},{2,18},{3,19},{4,20},{5,21},{6,22},{7,23},{8,24},{9,... | collective-permute-start | bytes 196616 | tf_op jit(solution)/shard_map/ppermute | solution.py:481
  101.7 5.5 %collective-permute-start.18 = (f32[32,512]{1,0:T(8,128)S(1)}, f32[32,512]{1,0:T(8,128)S(1)}, u32[]{:S(2)}, u32[]{:S(2)}) collective-permute-start(f32[32,512]{1,0:T(8,128)S(1)} %add.482), channel_id=1, source_target_pairs={{0,3},{1,2},{2,1},{3,0},{4,7},{5,6},{6,5},{7,4},{8,11},{9,10},{10,... | collective-permute-start | bytes 196616 | tf_op jit(solution)/shard_map/ppermute | solution.py:481
  115.9 6.0 %collective-permute-start.21 = (f32[4,32,512]{2,1,0:T(8,128)S(1)}, f32[4,32,512]{2,1,0:T(8,128)S(1)}, u32[]{:S(2)}, u32[]{:S(2)}) collective-permute-start(f32[4,32,512]{2,1,0:T(8,128)S(1)} %pad_maximum_fusion.2), channel_id=1, source_target_pairs={{0,16},{1,17},{2,18},{3,19},{4,20},{5,21},{6,22},{7,23},{8,24},{9,... | collective-permute-start | bytes 786440 | tf_op jit(solution)/shard_map/ppermute | solution.py:481
  121.9 56.4 %collective-permute-start.31 = (bf16[2048,1024]{1,0:T(8,128)(2,1)}, bf16[2048,1024]{1,0:T(8,128)(2,1)}, u32[]{:S(2)}, u32[]{:S(2)}) collective-permute-start(bf16[2048,1024]{1,0:T(8,128)(2,1)} %tie.2.refs_3_.refs_2_), channel_id=1, source_target_pairs={{0,4},{1,5},{2,6},{3,7},{4,8},{5,9},{6,10},{7,11},{8,12},{9,13},{1... | collective-permute-start | bytes 12582920 | tf_op jit(solution)/shard_map/ppermute | solution.py:481
  131.7 9.0 %collective-permute-start.26 = (f32[2,32,256]{2,1,0:T(8,128)S(1)}, f32[2,32,256]{2,1,0:T(8,128)S(1)}, u32[]{:S(2)}, u32[]{:S(2)}) collective-permute-start(f32[2,32,256]{2,1,0:T(8,128)S(1)} %constant_dynamic-update-slice_fusion.a), channel_id=1, source_target_pairs={{0,3},{1,2},{2,1},{3,0},{4,7},{5,6},{6,5},{7,4},{8,11},{9,10},{10,... | collective-permute-start | bytes 196616 | tf_op jit(solution)/shard_map/ppermute | solution.py:481
  140.8 20.4 %collective-permute-start.27 = (f32[4,32,256]{2,1,0:T(8,128)S(1)}, f32[4,32,256]{2,1,0:T(8,128)S(1)}, u32[]{:S(2)}, u32[]{:S(2)}) collective-permute-start(f32[4,32,256]{2,1,0:T(8,128)S(1)} %pair.2), channel_id=1, source_target_pairs={{0,16},{1,17},{2,18},{3,19},{4,20},{5,21},{6,22},{7,23},{8,24},{9,... | collective-permute-start | bytes 393224 | tf_op jit(solution)/shard_map/ppermute | solution.py:481
  147.4 72.1 %collective-permute-start.28 = (bf16[2048,1024]{1,0:T(8,128)(2,1)}, bf16[2048,1024]{1,0:T(8,128)(2,1)}, u32[]{:S(2)}, u32[]{:S(2)}) collective-permute-start(bf16[2048,1024]{1,0:T(8,128)(2,1)} %line.3.rest_0_.refs_1_), channel_id=1, source_target_pairs={{0,4},{1,5},{2,6},{3,7},{4,8},{5,9},{6,10},{7,11},{8,12},{9,13},{1... | collective-permute-start | bytes 12582920 | tf_op jit(solution)/shard_map/ppermute | solution.py:481
  161.8 57.7 %collective-permute-start.29 = (bf16[2048,1024]{1,0:T(8,128)(2,1)}, bf16[2048,1024]{1,0:T(8,128)(2,1)}, u32[]{:S(2)}, u32[]{:S(2)}) collective-permute-start(bf16[2048,1024]{1,0:T(8,128)(2,1)} %tie.3.refs_2_), channel_id=1, source_target_pairs={{0,12},{1,13},{2,14},{3,15},{4,0},{5,1},{6,2},{7,3},{8,4},{9,5},{1... | collective-permute-start | bytes 12582920 | tf_op jit(solution)/shard_map/ppermute | solution.py:481
  162.5 15.8 %collective-permute-start.30 = (f32[4,32,256]{2,1,0:T(8,128)}, f32[4,32,256]{2,1,0:T(8,128)S(1)}, u32[]{:S(2)}, u32[]{:S(2)}) collective-permute-start(f32[4,32,256]{2,1,0:T(8,128)} %copy-done.24), channel_id=1, source_target_pairs={{0,1},{1,0},{2,3},{3,2},{4,5},{5,4},{6,7},{7,6},{8,9},{9,8},{10,11... | collective-permute-start | bytes 393224 | tf_op jit(solution)/shard_map/ppermute | solution.py:481
  180.2 9.7 %collective-permute-start.32 = (f32[8,32,256]{2,1,0:T(8,128)S(1)}, f32[8,32,256]{2,1,0:T(8,128)S(1)}, u32[]{:S(2)}, u32[]{:S(2)}) collective-permute-start(f32[8,32,256]{2,1,0:T(8,128)S(1)} %pair.3), channel_id=1, source_target_pairs={{0,3},{1,2},{2,1},{3,0},{4,7},{5,6},{6,5},{7,4},{8,11},{9,10},{10,... | collective-permute-start | bytes 786440 | tf_op jit(solution)/shard_map/ppermute | solution.py:481
  (41 other events, 252.9 us)

commit v4 on v3

--- a/solution.py
+++ b/solution.py
@@ -559,7 +559,7 @@
     bottom1 = tie(bottom1, w, sum0)
     opposite1 = send(bottom1, QDOWN)
     sum1 = add_rows(errors, PART // STRIP, ((line1, 0), (bottom1, 2)), kept, 0, PART)
-    w = pair(w, send(w, PIN), part, sum0, sum1, opposite0)
+    w = pair(w, send(w, PIN), part, sum0, opposite0)
     w = cat(w, send(w, POUT))
     right = right_terms(in_kept, w, part, inverse, kept)
     for perm in (CORE, XIN, XOUT):

time: 230 us -> 230 us (level)
  waiting for transfers between devices: 69.9 us -> 74.8 us
  starting transfers between devices: 56.1 us -> 53.8 us
    ppermute x36, waiting for transfers between devices: 69.9 us -> 74.8 us  [send(): return lax.ppermute(a, ALL, perm)]
    unnamed x59 -> x53, local copies, waits for them, and re-layouts: 26 us -> 23.7 us
where the time goes in v4:
time: 230 us; the launch traced here: 229 us
  waiting for transfers between devices  74.8 us (33%)
  Pallas kernels  71.6 us (31%)
  starting transfers between devices  53.8 us (23%)
  local copies, waits for them, and re-layouts  27.4 us (12%)
    ppermute x36, waiting for transfers between devices, send(): return lax.ppermute(a, ALL, perm)  74.8 us
    pallas_call x15, Pallas kernels, kernel_call(): return lambda *args: call(*args, *after)  71.5 us
    ppermute x36, starting transfers between devices, send(): return lax.ppermute(a, ALL, perm)  53.8 us
    unnamed x53, local copies, waits for them, and re-layouts  23.7 us
  transfers between devices with their start and end apart: 36, of which 21 were waited for; matrix products, arithmetic and copies ran while one was open for 2% of the time, Pallas kernels for 26%

profile of v4, /device:TPU:1, one launch (start us, length us, event | category | flops | bytes accessed | tf_op | source)
XLA Modules:
  0.0 229.0 jit_solution(4661079726720383348)
XLA Ops:
  3.4 4.7 %collective-permute-start.1 = (bf16[4096,256]{1,0:T(8,128)(2,1)S(1)}, bf16[4096,256]{1,0:T(8,128)(2,1)}, u32[]{:S(2)}, u32[]{:S(2)}) collective-permute-start(bf16[4096,256]{1,0:T(8,128)(2,1)S(1)} %turn.1.refs_0_), channel_id=1, source_target_pairs={{0,3},{1,0},{2,1},{3,2},{4,7},{5,4},{6,5},{7,6},{8,11},{9,8},{10,9... | collective-permute-start | bytes 6291464 | tf_op jit(solution)/shard_map/ppermute | solution.py:481
  16.3 9.5 %errors_left.1.rest_0_.refs_2_ = f32[8,32,512]{2,1,0:T(8,128)} custom-call(s32[8]{0:T(128)} %stack.184.refs_0_, f32[32,512]{1,0:T(8,128)} %bitcast.75, f32[4096,512]{1,0:T(8,128)} %bitcast.70), custom_call_target="tpu_custom_call" | custom-call | tf_op jit(solution)/shard_map/errors_left/pallas_call | solution.py:107
  27.1 6.7 %collective-permute-done.1.refs_2_ = bf16[4096,256]{1,0:T(8,128)(2,1)} collective-permute-done((bf16[4096,256]{1,0:T(8,128)(2,1)S(1)}, bf16[4096,256]{1,0:T(8,128)(2,1)}, u32[]{:S(2)}, u32[]{:S(2)}) %collective-permute-start.1) | collective-permute-done | bytes 2097184 | tf_op jit(solution)/shard_map/ppermute | solution.py:481
  35.2 3.6 %collective-permute-start.2 = (bf16[2048,256]{1,0:T(8,128)(2,1)S(1)}, bf16[2048,256]{1,0:T(8,128)(2,1)S(1)}, u32[]{:S(2)}, u32[]{:S(2)}) collective-permute-start(bf16[2048,256]{1,0:T(8,128)(2,1)S(1)} %slice.56), channel_id=1, source_target_pairs={{0,3},{1,0},{2,1},{3,2},{4,7},{5,4},{6,5},{7,6},{8,11},{9,8},{10,9... | collective-permute-start | bytes 3145736 | tf_op jit(solution)/shard_map/ppermute | solution.py:481
  47.7 3.0 %collective-permute-done.7 = f32[32,256]{1,0:T(8,128)S(1)} collective-permute-done((f32[32,256]{1,0:T(8,128)S(1)}, f32[32,256]{1,0:T(8,128)S(1)}, u32[]{:S(2)}, u32[]{:S(2)}) %collective-permute-start.7) | collective-permute-done | bytes 32800 | tf_op jit(solution)/shard_map/ppermute | solution.py:481
  70.7 4.4 %line.3.rest_0_.refs_1_ = bf16[2048,1024]{1,0:T(8,128)(2,1)} custom-call(bf16[4096,256]{1,0:T(8,128)(2,1)S(1)} %copy-done.17, bf16[4096,256]{1,0:T(8,128)(2,1)} %collective-permute-done.refs_1_, bf16[4096,256]{1,0:T(8,128)(2,1)} %collective-permute-done.1.refs_2_, bf16[2048,256]{1,0:T(8,128)(2,1)S(1)} %collective-permute-done.2.refs_5_.refs_3_, ...), custom_call_target="tpu_custom_call" | custom-call | tf_op jit(solution)/shard_map/line/pallas_call | solution.py:107
  75.3 3.4 %collective-permute-done.13.r = f32[1,32,512]{2,1,0:T(8,128)S(1)} collective-permute-done((f32[1,32,512]{2,1,0:T(8,128)S(1)}, f32[1,32,512]{2,1,0:T(8,128)S(1)}, u32[]{:S(2)}, u32[]{:S(2)}) %collective-permute-start.13) | collective-permute-done | bytes 65568 | tf_op jit(solution)/shard_map/ppermute | solution.py:481
  84.5 3.9 %collective-permute-start.15 = (f32[32,512]{1,0:T(8,128)S(1)}, f32[32,512]{1,0:T(8,128)S(1)}, u32[]{:S(2)}, u32[]{:S(2)}) collective-permute-start(f32[32,512]{1,0:T(8,128)S(1)} %bitcast_add_fusion), channel_id=1, source_target_pairs={{0,3},{1,2},{2,1},{3,0},{4,7},{5,6},{6,5},{7,4},{8,11},{9,10},{10,... | collective-permute-start | bytes 196616 | tf_op jit(solution)/shard_map/ppermute | solution.py:481
  91.1 5.5 %collective-permute-start.16 = (f32[32,512]{1,0:T(8,128)S(1)}, f32[32,512]{1,0:T(8,128)S(1)}, u32[]{:S(2)}, u32[]{:S(2)}) collective-permute-start(f32[32,512]{1,0:T(8,128)S(1)} %add.481), channel_id=1, source_target_pairs={{0,16},{1,17},{2,18},{3,19},{4,20},{5,21},{6,22},{7,23},{8,24},{9,... | collective-permute-start | bytes 196616 | tf_op jit(solution)/shard_map/ppermute | solution.py:481
  97.5 4.3 %collective-permute-done.17 = f32[32,512]{1,0:T(8,128)S(1)} collective-permute-done((f32[32,512]{1,0:T(8,128)S(1)}, f32[32,512]{1,0:T(8,128)S(1)}, u32[]{:S(2)}, u32[]{:S(2)}) %collective-permute-start.17) | collective-permute-done | bytes 65568 | tf_op jit(solution)/shard_map/ppermute | solution.py:481
  102.0 5.3 %collective-permute-done.18 = f32[32,512]{1,0:T(8,128)S(1)} collective-permute-done((f32[32,512]{1,0:T(8,128)S(1)}, f32[32,512]{1,0:T(8,128)S(1)}, u32[]{:S(2)}, u32[]{:S(2)}) %collective-permute-start.18) | collective-permute-done | bytes 65568 | tf_op jit(solution)/shard_map/ppermute | solution.py:481
  107.3 3.5 %collective-permute-done.19 = f32[1,32,512]{2,1,0:T(8,128)S(1)} collective-permute-done((f32[1,32,512]{2,1,0:T(8,128)S(1)}, f32[1,32,512]{2,1,0:T(8,128)S(1)}, u32[]{:S(2)}, u32[]{:S(2)}) %collective-permute-start.19) | collective-permute-done | bytes 65568 | tf_op jit(solution)/shard_map/ppermute | solution.py:481
  116.0 3.9 %collective-permute-start.21 = (f32[4,32,512]{2,1,0:T(8,128)S(1)}, f32[4,32,512]{2,1,0:T(8,128)S(1)}, u32[]{:S(2)}, u32[]{:S(2)}) collective-permute-start(f32[4,32,512]{2,1,0:T(8,128)S(1)} %pad_maximum_fusion.2), channel_id=1, source_target_pairs={{0,16},{1,17},{2,18},{3,19},{4,20},{5,21},{6,22},{7,23},{8,24},{9,... | collective-permute-start | bytes 786440 | tf_op jit(solution)/shard_map/ppermute | solution.py:481
  128.2 3.6 %collective-permute-done.25 = f32[1,32,256]{2,1,0:T(8,128)S(1)} collective-permute-done((f32[1,32,256]{2,1,0:T(8,128)S(1)}, f32[1,32,256]{2,1,0:T(8,128)S(1)}, u32[]{:S(2)}, u32[]{:S(2)}) %collective-permute-start.25) | collective-permute-done | bytes 32800 | tf_op jit(solution)/shard_map/ppermute | solution.py:481
  134.4 6.4 %basis.1 = (f32[32,4096]{1,0:T(8,128)}, bf16[4096,192]{1,0:T(8,128)(2,1)S(1)}, f32[32,32]{1,0:T(8,128)S(1)}) custom-call(s32[8]{0:T(128)S(1)} %copy-done.24, f32[8,32,512]{2,1,0:T(8,128)S(1)} %pad_maximum_fusion.refs_1_), custom_call_target="tpu_custom_call" | custom-call | tf_op jit(solution)/shard_map/basis/pallas_call | solution.py:107
  149.4 9.7 %add_rows.4.refs_2_.rest_1_.refs_0_ = f32[2048,512]{1,0:T(8,128)S(1)} custom-call(f32[4096,512]{1,0:T(8,128)} %bitcast.71, bf16[2048,1024]{1,0:T(8,128)(2,1)S(1)} %copy-done.10, bf16[2048,1024]{1,0:T(8,128)(2,1)S(1)} %copy-done.13, bf16[2048,1024]{1,0:T(8,128)(2,1)} %collective-permute-done.23.refs_2_.refs_4_.refs_3_, bf16[4096,512]{1,0:T(8,128)(2,1)} %copy-done, ...), custom_call_target="tpu_custom_call" | custom-call | tf_op jit(solution)/shard_map/add_rows/pallas_call | solution.py:107
  162.6 3.4 %copy-done.5 = f32[1,4096,512]{2,1,0:T(8,128)S(1)} copy-done((f32[1,4096,512]{2,1,0:T(8,128)S(1)}, f32[1,4096,512]{2,1,0:T(8,128)}, u32[]{:S(2)}) %copy-start.5) | copy-done | bytes 8388632
  166.0 4.1 %errors_right.1.rest_0_.refs_2_ = f32[32,512]{1,0:T(8,128)S(1)} custom-call(s32[8]{0:T(128)S(1)} %copy-done.24, f32[8,32,512]{2,1,0:T(8,128)S(1)} %pad_maximum_fusion.refs_1_, f32[4096,512]{1,0:T(8,128)S(1)} %bitcast.73), custom_call_target="tpu_custom_call" | custom-call | tf_op jit(solution)/shard_map/errors_right/pallas_call | solution.py:107
  172.6 9.1 %collective-permute-done.32 = f32[8,32,256]{2,1,0:T(8,128)S(1)} collective-permute-done((f32[8,32,256]{2,1,0:T(8,128)S(1)}, f32[8,32,256]{2,1,0:T(8,128)S(1)}, u32[]{:S(2)}, u32[]{:S(2)}) %collective-permute-start.32) | collective-permute-done | bytes 262176 | tf_op jit(solution)/shard_map/ppermute | solution.py:481
  188.6 3.5 %collective-permute-done.34 = f32[32,512]{1,0:T(8,128)S(1)} collective-permute-done((f32[32,512]{1,0:T(8,128)S(1)}, f32[32,512]{1,0:T(8,128)S(1)}, u32[]{:S(2)}, u32[]{:S(2)}) %collective-permute-start.34) | collective-permute-done | bytes 65568 | tf_op jit(solution)/shard_map/ppermute | solution.py:481
  194.7 7.7 %add_rows.5.refs_0_ = f32[2048,512]{1,0:T(8,128)S(1)} custom-call(f32[4096,512]{1,0:T(8,128)} %bitcast.72, bf16[2048,1024]{1,0:T(8,128)(2,1)} %line.3.rest_0_.refs_1_, bf16[2048,1024]{1,0:T(8,128)(2,1)} %tie.3.refs_2_, bf16[4096,512]{1,0:T(8,128)(2,1)S(1)} %copy-done.2, bf16[4096,512]{1,0:T(8,128)(2,1)S(1)} %copy-done.2), custom_call_target="tpu_custom_call" | custom-call | tf_op jit(solution)/shard_map/add_rows/pallas_call | solution.py:107
  202.4 6.5 %add_rows.6.refs_7_ = f32[4096,512]{1,0:T(8,128)} custom-call(f32[2048,512]{1,0:T(8,128)S(1)} %copy-done.8, bf16[2048,1024]{1,0:T(8,128)(2,1)} %collective-permute-done.31.rest_2_.refs_1_, bf16[4096,512]{1,0:T(8,128)(2,1)S(1)} %copy-done.2, bf16[4096,192]{1,0:T(8,128)(2,1)S(1)} %get-tuple-element.7.refs_3_.refs_5_, f32[32,512]{1,0:T(8,128)S(1)} %add.549.refs_4_.refs_6_), custom_call_target="tpu_custom_call" | custom-call | tf_op jit(solution)/shard_map/add_rows/pallas_call | solution.py:107
  208.9 10.7 %collective-permute-done.28.refs_1_ = bf16[2048,1024]{1,0:T(8,128)(2,1)} collective-permute-done((bf16[2048,1024]{1,0:T(8,128)(2,1)}, bf16[2048,1024]{1,0:T(8,128)(2,1)}, u32[]{:S(2)}, u32[]{:S(2)}) %collective-permute-start.28) | collective-permute-done | bytes 4194336 | tf_op jit(solution)/shard_map/ppermute | solution.py:481
  219.6 9.4 %add_rows.7 = f32[4096,512]{1,0:T(8,128)} custom-call(f32[2048,512]{1,0:T(8,128)S(1)} %add_rows.5.refs_0_, bf16[2048,1024]{1,0:T(8,128)(2,1)} %collective-permute-done.28.refs_1_, bf16[2048,1024]{1,0:T(8,128)(2,1)} %collective-permute-done.29.refs_2_, bf16[4096,512]{1,0:T(8,128)(2,1)} %copy-done, ...), custom_call_target="tpu_custom_call", output_to_operand_aliasing={{}: (7, {})} | custom-call | tf_op jit(solution)/shard_map/add_rows/pallas_call | solution.py:107
  (152 shorter events, 92.1 us)
Async XLA Ops:
  3.4 30.4 %collective-permute-start.1 = (bf16[4096,256]{1,0:T(8,128)(2,1)S(1)}, bf16[4096,256]{1,0:T(8,128)(2,1)}, u32[]{:S(2)}, u32[]{:S(2)}) collective-permute-start(bf16[4096,256]{1,0:T(8,128)(2,1)S(1)} %turn.1.refs_0_), channel_id=1, source_target_pairs={{0,3},{1,0},{2,1},{3,2},{4,7},{5,4},{6,5},{7,6},{8,11},{9,8},{10,9... | collective-permute-start | bytes 6291464 | tf_op jit(solution)/shard_map/ppermute | solution.py:481
  8.1 30.7 %collective-permute-start = (bf16[4096,256]{1,0:T(8,128)(2,1)S(1)}, bf16[4096,256]{1,0:T(8,128)(2,1)}, u32[]{:S(2)}, u32[]{:S(2)}) collective-permute-start(bf16[4096,256]{1,0:T(8,128)(2,1)S(1)} %turn.1.refs_0_), channel_id=1, source_target_pairs={{0,1},{1,2},{2,3},{3,0},{4,5},{5,6},{6,7},{7,4},{8,9},{9,10},{10,1... | collective-permute-start | bytes 6291464 | tf_op jit(solution)/shard_map/ppermute | solution.py:481
  12.8 13.0 %collective-permute-start.3 = (f32[8,32,256]{2,1,0:T(8,128)S(1)}, f32[8,32,256]{2,1,0:T(8,128)S(1)}, u32[]{:S(2)}, u32[]{:S(2)}) collective-permute-start(f32[8,32,256]{2,1,0:T(8,128)S(1)} %slice.57), channel_id=1, source_target_pairs={{0,12},{1,13},{2,14},{3,15},{4,8},{5,9},{6,10},{7,11},{8,4},{9,5},... | collective-permute-start | bytes 786440 | tf_op jit(solution)/shard_map/ppermute | solution.py:481
  27.0 13.1 %collective-permute-start.4 = (f32[4,32,256]{2,1,0:T(8,128)S(1)}, f32[4,32,256]{2,1,0:T(8,128)S(1)}, u32[]{:S(2)}, u32[]{:S(2)}) collective-permute-start(f32[4,32,256]{2,1,0:T(8,128)S(1)} %slice.59), channel_id=1, source_target_pairs={{0,4},{1,5},{2,6},{3,7},{4,0},{5,1},{6,2},{7,3},{8,12},{9,13},{10,... | collective-permute-start | bytes 393224 | tf_op jit(solution)/shard_map/ppermute | solution.py:481
  35.2 18.4 %collective-permute-start.2 = (bf16[2048,256]{1,0:T(8,128)(2,1)S(1)}, bf16[2048,256]{1,0:T(8,128)(2,1)S(1)}, u32[]{:S(2)}, u32[]{:S(2)}) collective-permute-start(bf16[2048,256]{1,0:T(8,128)(2,1)S(1)} %slice.56), channel_id=1, source_target_pairs={{0,3},{1,0},{2,1},{3,2},{4,7},{5,4},{6,5},{7,6},{8,11},{9,8},{10,9... | collective-permute-start | bytes 3145736 | tf_op jit(solution)/shard_map/ppermute | solution.py:481
  40.1 15.9 %collective-permute-start.9 = (bf16[2048,256]{1,0:T(8,128)(2,1)S(1)}, bf16[2048,256]{1,0:T(8,128)(2,1)S(1)}, u32[]{:S(2)}, u32[]{:S(2)}) collective-permute-start(bf16[2048,256]{1,0:T(8,128)(2,1)S(1)} %slice.64), channel_id=1, source_target_pairs={{0,1},{1,2},{2,3},{3,0},{4,5},{5,6},{6,7},{7,4},{8,9},{9,10},{10,1... | collective-permute-start | bytes 3145736 | tf_op jit(solution)/shard_map/ppermute | solution.py:481
  42.0 5.6 %collective-permute-start.6 = (f32[2,32,256]{2,1,0:T(8,128)S(1)}, f32[2,32,256]{2,1,0:T(8,128)S(1)}, u32[]{:S(2)}, u32[]{:S(2)}) collective-permute-start(f32[2,32,256]{2,1,0:T(8,128)S(1)} %slice.61), channel_id=1, source_target_pairs={{0,12},{1,13},{2,14},{3,15},{4,8},{5,9},{6,10},{7,11},{8,4},{9,5},... | collective-permute-start | bytes 196616 | tf_op jit(solution)/shard_map/ppermute | solution.py:481
  50.8 7.8 %collective-permute-start.8 = (f32[32,256]{1,0:T(8,128)S(1)}, f32[32,256]{1,0:T(8,128)S(1)}, u32[]{:S(2)}, u32[]{:S(2)}) collective-permute-start(f32[32,256]{1,0:T(8,128)S(1)} %fusion.refs_4_), channel_id=1, source_target_pairs={{0,16},{1,17},{2,18},{3,19},{4,20},{5,21},{6,22},{7,23},{8,24},{9,... | collective-permute-start | bytes 98312 | tf_op jit(solution)/shard_map/ppermute | solution.py:481
  62.5 57.4 %collective-permute-start.22 = (bf16[2048,1024]{1,0:T(8,128)(2,1)S(1)}, bf16[2048,1024]{1,0:T(8,128)(2,1)S(1)}, u32[]{:S(2)}, u32[]{:S(2)}) collective-permute-start(bf16[2048,1024]{1,0:T(8,128)(2,1)S(1)} %line.2.refs_4_.refs_1_), channel_id=1, source_target_pairs={{0,4},{1,5},{2,6},{3,7},{4,8},{5,9},{6,10},{7,11},{8,12},{9,13},{1... | collective-permute-start | bytes 12582920 | tf_op jit(solution)/shard_map/ppermute | solution.py:481
  62.5 59.4 %collective-permute-start.23 = (bf16[2048,1024]{1,0:T(8,128)(2,1)S(1)}, bf16[2048,1024]{1,0:T(8,128)(2,1)}, u32[]{:S(2)}, u32[]{:S(2)}) collective-permute-start(bf16[2048,1024]{1,0:T(8,128)(2,1)S(1)} %line.2.refs_4_.refs_1_), channel_id=1, source_target_pairs={{0,12},{1,13},{2,14},{3,15},{4,0},{5,1},{6,2},{7,3},{8,4},{9,5},{1... | collective-permute-start | bytes 12582920 | tf_op jit(solution)/shard_map/ppermute | solution.py:481
  75.1 86.1 %collective-permute-start.12 = (bf16[2048,1024]{1,0:T(8,128)(2,1)}, bf16[2048,1024]{1,0:T(8,128)(2,1)}, u32[]{:S(2)}, u32[]{:S(2)}) collective-permute-start(bf16[2048,1024]{1,0:T(8,128)(2,1)} %line.3.rest_0_.refs_1_), channel_id=1, source_target_pairs={{0,12},{1,13},{2,14},{3,15},{4,0},{5,1},{6,2},{7,3},{8,4},{9,5},{1... | collective-permute-start | bytes 12582920 | tf_op jit(solution)/shard_map/ppermute | solution.py:481
  78.7 5.7 %collective-permute-start.14 = (f32[32,512]{1,0:T(8,128)S(1)}, f32[32,512]{1,0:T(8,128)S(1)}, u32[]{:S(2)}, u32[]{:S(2)}) collective-permute-start(f32[32,512]{1,0:T(8,128)S(1)} %bitcast.77), channel_id=1, source_target_pairs={{0,1},{1,0},{2,3},{3,2},{4,5},{5,4},{6,7},{7,6},{8,9},{9,8},{10,11... | collective-permute-start | bytes 196616 | tf_op jit(solution)/shard_map/ppermute | solution.py:481
  84.5 6.6 %collective-permute-start.15 = (f32[32,512]{1,0:T(8,128)S(1)}, f32[32,512]{1,0:T(8,128)S(1)}, u32[]{:S(2)}, u32[]{:S(2)}) collective-permute-start(f32[32,512]{1,0:T(8,128)S(1)} %bitcast_add_fusion), channel_id=1, source_target_pairs={{0,3},{1,2},{2,1},{3,0},{4,7},{5,6},{6,5},{7,4},{8,11},{9,10},{10,... | collective-permute-start | bytes 196616 | tf_op jit(solution)/shard_map/ppermute | solution.py:481
  91.1 6.4 %collective-permute-start.16 = (f32[32,512]{1,0:T(8,128)S(1)}, f32[32,512]{1,0:T(8,128)S(1)}, u32[]{:S(2)}, u32[]{:S(2)}) collective-permute-start(f32[32,512]{1,0:T(8,128)S(1)} %add.481), channel_id=1, source_target_pairs={{0,16},{1,17},{2,18},{3,19},{4,20},{5,21},{6,22},{7,23},{8,24},{9,... | collective-permute-start | bytes 196616 | tf_op jit(solution)/shard_map/ppermute | solution.py:481
  101.8 5.5 %collective-permute-start.18 = (f32[32,512]{1,0:T(8,128)S(1)}, f32[32,512]{1,0:T(8,128)S(1)}, u32[]{:S(2)}, u32[]{:S(2)}) collective-permute-start(f32[32,512]{1,0:T(8,128)S(1)} %add.482), channel_id=1, source_target_pairs={{0,3},{1,2},{2,1},{3,0},{4,7},{5,6},{6,5},{7,4},{8,11},{9,10},{10,... | collective-permute-start | bytes 196616 | tf_op jit(solution)/shard_map/ppermute | solution.py:481
  116.0 6.0 %collective-permute-start.21 = (f32[4,32,512]{2,1,0:T(8,128)S(1)}, f32[4,32,512]{2,1,0:T(8,128)S(1)}, u32[]{:S(2)}, u32[]{:S(2)}) collective-permute-start(f32[4,32,512]{2,1,0:T(8,128)S(1)} %pad_maximum_fusion.2), channel_id=1, source_target_pairs={{0,16},{1,17},{2,18},{3,19},{4,20},{5,21},{6,22},{7,23},{8,24},{9,... | collective-permute-start | bytes 786440 | tf_op jit(solution)/shard_map/ppermute | solution.py:481
  121.9 49.9 %collective-permute-start.31 = (bf16[2048,1024]{1,0:T(8,128)(2,1)}, bf16[2048,1024]{1,0:T(8,128)(2,1)}, u32[]{:S(2)}, u32[]{:S(2)}) collective-permute-start(bf16[2048,1024]{1,0:T(8,128)(2,1)} %tie.2.refs_3_.refs_2_), channel_id=1, source_target_pairs={{0,4},{1,5},{2,6},{3,7},{4,8},{5,9},{6,10},{7,11},{8,12},{9,13},{1... | collective-permute-start | bytes 12582920 | tf_op jit(solution)/shard_map/ppermute | solution.py:481
  131.7 9.0 %collective-permute-start.26 = (f32[2,32,256]{2,1,0:T(8,128)S(1)}, f32[2,32,256]{2,1,0:T(8,128)S(1)}, u32[]{:S(2)}, u32[]{:S(2)}) collective-permute-start(f32[2,32,256]{2,1,0:T(8,128)S(1)} %constant_dynamic-update-slice_fusion.a), channel_id=1, source_target_pairs={{0,3},{1,2},{2,1},{3,0},{4,7},{5,6},{6,5},{7,4},{8,11},{9,10},{10,... | collective-permute-start | bytes 196616 | tf_op jit(solution)/shard_map/ppermute | solution.py:481
  140.8 20.4 %collective-permute-start.27 = (f32[4,32,256]{2,1,0:T(8,128)S(1)}, f32[4,32,256]{2,1,0:T(8,128)S(1)}, u32[]{:S(2)}, u32[]{:S(2)}) collective-permute-start(f32[4,32,256]{2,1,0:T(8,128)S(1)} %pair.2), channel_id=1, source_target_pairs={{0,16},{1,17},{2,18},{3,19},{4,20},{5,21},{6,22},{7,23},{8,24},{9,... | collective-permute-start | bytes 393224 | tf_op jit(solution)/shard_map/ppermute | solution.py:481
  147.4 72.1 %collective-permute-start.28 = (bf16[2048,1024]{1,0:T(8,128)(2,1)}, bf16[2048,1024]{1,0:T(8,128)(2,1)}, u32[]{:S(2)}, u32[]{:S(2)}) collective-permute-start(bf16[2048,1024]{1,0:T(8,128)(2,1)} %line.3.rest_0_.refs_1_), channel_id=1, source_target_pairs={{0,4},{1,5},{2,6},{3,7},{4,8},{5,9},{6,10},{7,11},{8,12},{9,13},{1... | collective-permute-start | bytes 12582920 | tf_op jit(solution)/shard_map/ppermute | solution.py:481
  161.8 57.7 %collective-permute-start.29 = (bf16[2048,1024]{1,0:T(8,128)(2,1)}, bf16[2048,1024]{1,0:T(8,128)(2,1)}, u32[]{:S(2)}, u32[]{:S(2)}) collective-permute-start(bf16[2048,1024]{1,0:T(8,128)(2,1)} %tie.3.refs_2_), channel_id=1, source_target_pairs={{0,12},{1,13},{2,14},{3,15},{4,0},{5,1},{6,2},{7,3},{8,4},{9,5},{1... | collective-permute-start | bytes 12582920 | tf_op jit(solution)/shard_map/ppermute | solution.py:481
  162.6 7.5 %collective-permute-start.30 = (f32[4,32,256]{2,1,0:T(8,128)}, f32[4,32,256]{2,1,0:T(8,128)S(1)}, u32[]{:S(2)}, u32[]{:S(2)}) collective-permute-start(f32[4,32,256]{2,1,0:T(8,128)} %copy-done.21), channel_id=1, source_target_pairs={{0,1},{1,0},{2,3},{3,2},{4,5},{5,4},{6,7},{7,6},{8,9},{9,8},{10,11... | collective-permute-start | bytes 393224 | tf_op jit(solution)/shard_map/ppermute | solution.py:481
  171.8 9.8 %collective-permute-start.32 = (f32[8,32,256]{2,1,0:T(8,128)S(1)}, f32[8,32,256]{2,1,0:T(8,128)S(1)}, u32[]{:S(2)}, u32[]{:S(2)}) collective-permute-start(f32[8,32,256]{2,1,0:T(8,128)S(1)} %pair.3), channel_id=1, source_target_pairs={{0,3},{1,2},{2,1},{3,0},{4,7},{5,6},{6,5},{7,4},{8,11},{9,10},{10,... | collective-permute-start | bytes 786440 | tf_op jit(solution)/shard_map/ppermute | solution.py:481
  192.1 10.2 %collective-permute-start.35 = (f32[32,512]{1,0:T(8,128)S(1)}, f32[32,512]{1,0:T(8,128)S(1)}, u32[]{:S(2)}, u32[]{:S(2)}) collective-permute-start(f32[32,512]{1,0:T(8,128)S(1)} %add.548), channel_id=1, source_target_pairs={{0,96},{1,97},{2,98},{3,99},{4,100},{5,101},{6,102},{7,103},{8,104... | collective-permute-start | bytes 196616 | tf_op jit(solution)/shard_map/ppermute | solution.py:481
  (38 other events, 222.3 us)
